TPU v7x, 512 devices: a whole 4x4x16 slice. The times are simulated.
512 devices in a mesh: depth: 4 (over z_lo), row: 8 (over z_hi, core), col: 16 (over x, y).
Axes of the slice: x: 4, y: 4, z: 16 (z_hi: 4, z_lo: 4; z = z_hi * 4 + z_lo), core: 2. Of those that a mesh axis runs over, the one named last changes fastest.
Arguments:
- pair: bfloat16 [384, 384, 128], P('row', 'col'), may hold values from -6 to 6
- cotangent: bfloat16 [384, 384, 128], P('row', 'col'), may hold values from -6 to 6
- w_in: bfloat16 [128, 512], replicated, may hold values from -0.5 to 0.5
- w_gate: bfloat16 [128, 128], replicated, may hold values from -0.5 to 0.5
- w_out: bfloat16 [128, 128], replicated, may hold values from -0.5 to 0.5
- residue_mask: int32 [384], replicated, may hold values 0 or 1
Outputs:
- update: bfloat16 [384, 384, 128], P('row', 'col')
- pair_grad: bfloat16 [384, 384, 128], P('row', 'col')
All inputs are finite; a program needn't handle non-finite values.
Results may differ from a plain program's by a relative error of at most 0.024.
Values may be sent and summed in bfloat16 or wider, within the bound.
A program may use at most 64 MiB of HBM per device.

v0:
```python
import jax
import jax.numpy as jnp
from jax import lax
from jax.sharding import PartitionSpec as P


def from_root(value, axis, source):
    kept = jnp.where(lax.axis_index(axis) == source, value, 0).astype(value.dtype)
    return lax.psum(kept, axis)


def layer_norm(values):
    average = jnp.mean(values, axis=-1, keepdims=True)
    centered = values - average
    variance = jnp.mean(centered * centered, axis=-1, keepdims=True)
    inv_std = lax.rsqrt(variance + 1e-05)
    return (centered * inv_std, inv_std)


def norm_back(x_hat, inv_std, upstream):
    first = jnp.mean(upstream, axis=-1, keepdims=True)
    second = jnp.mean(upstream * x_hat, axis=-1, keepdims=True)
    return inv_std * (upstream - first - x_hat * second)


def finish(tri_sum, normed_rows, cot_rows, w_gate, w_out):
    y_hat, tri_std = layer_norm(tri_sum)
    y_norm = y_hat.astype(jnp.bfloat16)
    gate_val = jax.nn.sigmoid(
        jnp.einsum("ijc,cd->ijd", normed_rows, w_gate, preferred_element_type=jnp.float32)
    )
    out_proj = jnp.einsum("ijh,hc->ijc", y_norm, w_out, preferred_element_type=jnp.float32)
    update = (gate_val * out_proj).astype(jnp.bfloat16)
    cot_float = cot_rows.astype(jnp.float32)
    d_o = (cot_float * gate_val).astype(jnp.bfloat16)
    d_gate_pre = (cot_float * out_proj * gate_val * (1.0 - gate_val)).astype(jnp.bfloat16)
    d_y = jnp.einsum("ijc,hc->ijh", d_o, w_out, preferred_element_type=jnp.float32)
    tri_grad = norm_back(y_hat, tri_std, d_y).astype(jnp.bfloat16)
    d_gate = jnp.einsum("ijd,cd->ijc", d_gate_pre, w_gate, preferred_element_type=jnp.float32)
    return (update, tri_grad, d_gate)


def shards(pair, cotangent, w_in, w_gate, w_out, residue_mask):
    rows_t = pair.shape[0]
    cols_t = pair.shape[1]
    hidden = w_out.shape[0]
    depth_n = lax.axis_size("depth")
    sub_cols = cols_t // depth_n
    d_idx = lax.axis_index("depth")
    r_idx = lax.axis_index("row")
    c_idx = lax.axis_index("col")
    x_hat, inv_std = layer_norm(pair.astype(jnp.float32))
    normed = x_hat.astype(jnp.bfloat16)
    normed_sub = lax.dynamic_slice_in_dim(normed, d_idx * sub_cols, sub_cols, 1)
    projected = jnp.einsum("ijc,ce->ije", normed_sub, w_in, preferred_element_type=jnp.float32)
    mask_float = residue_mask.astype(jnp.float32)
    mask_rows = lax.dynamic_slice_in_dim(mask_float, r_idx * rows_t, rows_t, 0)
    mask_cols = lax.dynamic_slice_in_dim(mask_float, c_idx * cols_t + d_idx * sub_cols, sub_cols, 0)
    pair_mask = (mask_rows[:, None] * mask_cols[None, :])[..., None]
    sig_a = jax.nn.sigmoid(projected[..., :hidden])
    val_a = projected[..., hidden : 2 * hidden]
    sig_b = jax.nn.sigmoid(projected[..., 2 * hidden : 3 * hidden])
    val_b = projected[..., 3 * hidden :]
    a_sub = (pair_mask * sig_a * val_a).astype(jnp.bfloat16)
    b_sub = (pair_mask * sig_b * val_b).astype(jnp.bfloat16)
    a_panel, b_own = (
        lax.all_gather(a_sub, "col", axis=1, tiled=True),
        lax.all_gather(b_sub, "col", axis=1, tiled=True),
    )
    offset = c_idx * cols_t % rows_t
    b_piece = lax.dynamic_slice_in_dim(b_own, offset, cols_t, 0)
    b_panel = from_root(b_piece, "row", c_idx * cols_t // rows_t)
    partial_value = jnp.einsum("ikh,jkh->ijh", a_panel, b_panel, preferred_element_type=jnp.float32)
    tri_sum = lax.psum(partial_value.astype(jnp.bfloat16), "depth").astype(jnp.float32)
    update, tri_grad, d_gate = finish(tri_sum, normed, cotangent, w_gate, w_out)
    da_part = jnp.einsum("ijh,jkh->ikh", tri_grad, b_panel, preferred_element_type=jnp.float32)
    grad_a = lax.psum_scatter(
        da_part.astype(jnp.bfloat16), "col", scatter_dimension=1, tiled=True
    ).astype(jnp.float32)
    db_part = jnp.einsum("ijh,ikh->jkh", tri_grad, a_panel, preferred_element_type=jnp.float32)
    db_total = lax.psum(db_part.astype(jnp.bfloat16), "row").astype(jnp.float32)
    db_every = lax.all_to_all(
        db_total.astype(jnp.bfloat16), "col", split_axis=1, concat_axis=0, tiled=True
    ).astype(db_total.dtype)
    grad_b = lax.dynamic_slice_in_dim(db_every, r_idx * rows_t, rows_t, 0)
    d_projected = jnp.concatenate(
        [
            grad_a * pair_mask * val_a * sig_a * (1.0 - sig_a),
            grad_a * pair_mask * sig_a,
            grad_b * pair_mask * val_b * sig_b * (1.0 - sig_b),
            grad_b * pair_mask * sig_b,
        ],
        axis=-1,
    ).astype(jnp.bfloat16)
    dx_ab = jnp.einsum("ije,ce->ijc", d_projected, w_in, preferred_element_type=jnp.float32)
    dx_cols = lax.all_gather(dx_ab.astype(jnp.bfloat16), "depth", axis=1, tiled=True).astype(
        dx_ab.dtype
    )
    d_normed = dx_cols + d_gate
    pair_grad = norm_back(x_hat, inv_std, d_normed).astype(jnp.bfloat16)
    return (update, pair_grad)


def solution(mesh):
    in_specs = (P("row", "col", None), P("row", "col", None), P(), P(), P(), P())
    out_specs = (P("row", "col", None), P("row", "col", None))
    return jax.shard_map(shards, mesh=mesh, in_specs=in_specs, out_specs=out_specs, check_vma=False)
```

profile of v0, /device:TPU:24, one launch (start us, length us, event | category | flops | bytes accessed | tf_op | source)
XLA Modules:
  0.0 539.3 jit_solution(9421586949064447485)
XLA Ops:
  7.2 0.0 copy-start
  7.2 0.0 all-gather.3.cloned.1.call-start
  7.2 0.7 convert_element_type.85
  7.9 0.1 dynamic_slice.16
  8.0 0.1 dynamic_slice.15
  8.1 1.2 convert_reduce_fusion.1
  9.3 1.4 fusion.24
  10.7 1.3 fusion.19
  12.0 0.1 broadcast_multiply_fusion.6
  12.1 0.2 fusion.47
  12.3 0.0 copy-start.4
  12.3 0.8 copy-done.4
  13.1 0.8 multiply_convert_fusion.5
  13.9 0.0 all-gather.3.cloned.1.call-update
  13.9 0.0 all-gather.5.cloned.1.call-start
  14.0 0.7 all-gather.5.cloned.1.call-update
  14.7 0.0 all-reduce.4.cloned.1.call-start
  14.8 61.6 %all-gather.3.cloned.1.call-done = bf16[48,96,128]{2,0,1:T(8,128)(2,1)} async-done(((bf16[48,6,128]{2,0,1:T(8,128)(2,1)}), bf16[48,96,128]{2,0,1:T(8,128)(2,1)}) %all-gather.3.cloned.1.call-update) | async-done | bytes 1179664 | tf_op jit(solution)/shard_map/all_gather | solution.py:68
  76.3 1.3 constant_dynamic-slice_fusion
  77.7 0.0 copy-start.11
  77.7 0.6 copy.72
  78.3 0.9 broadcast_select_fusion
  79.2 0.0 all-reduce.4.cloned.1.call-update
  79.2 0.0 all-reduce.6.cloned.1.call-start
  79.3 1.2 fusion.14
  80.5 57.4 %all-gather.5.cloned.1.call-done = bf16[48,96,128]{2,0,1:T(8,128)(2,1)} async-done(((bf16[48,6,128]{2,0,1:T(8,128)(2,1)}), bf16[48,96,128]{2,0,1:T(8,128)(2,1)}) %all-gather.5.cloned.1.call-update) | async-done | bytes 1179664 | tf_op jit(solution)/shard_map/all_gather | solution.py:67
  137.8 5.3 copy.59
  143.1 0.0 copy-start.10
  143.2 100.5 %all-reduce.4.cloned.1.call-done = bf16[24,96,128]{1,0,2:T(8,128)(2,1)} async-done(((bf16[24,96,128]{1,0,2:T(8,128)(2,1)}), bf16[24,96,128]{1,0,2:T(8,128)(2,1)}) %all-reduce.4.cloned.1.call-update) | async-done | bytes 589840 | tf_op jit(solution)/shard_map/psum | solution.py:9
  243.6 3.0 fusion.10
  246.7 0.0 all-reduce.6.cloned.1.call-update
  246.7 0.0 all-reduce.8.cloned.1.call-start
  246.7 2.3 fusion.58
  249.1 0.1 copy.61
  249.1 2.7 copy.62
  251.8 60.0 %all-reduce.6.cloned.1.call-done = bf16[48,24,128]{0,1,2:T(8,128)(2,1)} async-done(((bf16[48,24,128]{0,1,2:T(8,128)(2,1)}), bf16[48,24,128]{0,1,2:T(8,128)(2,1)}) %all-reduce.6.cloned.1.call-update) | async-done | bytes 294928 | tf_op jit(solution)/shard_map/psum | solution.py:74
  311.9 1.5 convert_reduce_fusion
  313.4 1.5 fusion.9
  314.9 1.5 fusion.5
  316.4 1.4 fusion.8
  317.8 0.9 copy-done.3
  318.7 2.6 fusion.11
  321.3 0.0 all-reduce.8.cloned.1.call-update
  321.3 0.0 reduce-scatter.2.cloned.1.call-start
  321.4 2.0 fusion.59
  323.4 2.1 copy.64
  325.5 0.0 reduce-scatter.2.cloned.1.call-update
  325.6 0.0 copy-start.9
  325.6 98.3 %all-reduce.8.cloned.1.call-done = bf16[24,96,128]{1,0,2:T(8,128)(2,1)} async-done(((bf16[24,96,128]{1,0,2:T(8,128)(2,1)}), bf16[24,96,128]{1,0,2:T(8,128)(2,1)}) %all-reduce.8.cloned.1.call-update) | async-done | bytes 589840 | tf_op jit(solution)/shard_map/psum | solution.py:81
  423.9 2.6 copy.66
  426.4 7.2 %all-to-all-start = ((bf16[24,96,128]{2,0,1:T(8,128)(2,1)}), bf16[24,96,128]{2,0,1:T(8,128)(2,1)S(1)}, u32[]{:S(2)}, u32[]{:S(2)}) async-start(bf16[24,96,128]{2,0,1:T(8,128)(2,1)} %copy.66), calls=%async_computation.1 | async-start | bytes 1179648 | tf_op jit(solution)/shard_map/all_to_all | solution.py:82
  433.6 0.5 copy.60
  434.2 1.0 fusion.28
  435.2 7.8 %all-to-all-done = bf16[24,96,128]{2,0,1:T(8,128)(2,1)S(1)} async-done(((bf16[24,96,128]{2,0,1:T(8,128)(2,1)}), bf16[24,96,128]{2,0,1:T(8,128)(2,1)S(1)}, u32[]{:S(2)}, u32[]{:S(2)}) %all-to-all-start) | async-done | bytes 589856 | tf_op jit(solution)/shard_map/all_to_all | solution.py:82
  443.0 0.1 convert_bitcast_fusion
  443.1 0.1 copy.67
  443.2 0.0 copy-start.6
  443.2 70.7 %reduce-scatter.2.cloned.1.call-done = bf16[48,6,128]{2,0,1:T(8,128)(2,1)} async-done(((bf16[48,96,128]{2,0,1:T(8,128)(2,1)}), bf16[48,6,128]{2,0,1:T(8,128)(2,1)}) %reduce-scatter.2.cloned.1.call-update) | async-done | bytes 73744 | tf_op jit(solution)/shard_map/reduce_scatter | solution.py:77
  513.9 1.0 multiply_convert_fusion.4
  514.9 0.2 convolution_convert_fusion.2
  515.2 14.8 %all_gather.11 = bf16[48,24,128]{2,0,1:T(8,128)(2,1)S(1)} all-gather(bf16[48,6,128]{2,0,1:T(8,128)(2,1)S(1)} %convolution_convert_fusion.2), channel_id=1, replica_groups=mesh['depth'=4,'row'=8,'col'=16] {'depth'}, dimensions={1}, use_global_device_ids=true | all-gather | bytes 368640 | tf_op jit(solution)/shard_map/all_gather | solution.py:96
  529.9 0.9 fusion.57
  530.8 0.8 fusion.23
  531.7 0.8 copy.69
  (23 shorter events, 0.1 us)
Async XLA Ops:
  7.2 4.9 copy-start
  7.2 69.1 %all-gather.3.cloned.1.call-start = ((), (), s32[]{:S(2)}) async-start(), calls=%async_computation.2 | async-start | bytes 1253376 | tf_op jit(solution)/shard_map/all_gather | solution.py:68
  12.3 0.8 copy-start.4
  13.9 123.9 %all-gather.5.cloned.1.call-start = ((), (), s32[]{:S(2)}) async-start(), calls=%async_computation.4 | async-start | bytes 1253376 | tf_op jit(solution)/shard_map/all_gather | solution.py:67
  14.7 229.0 %all-reduce.4.cloned.1.call-start = ((), (), s32[]{:S(2)}) async-start(), calls=%async_computation.3 | async-start | bytes 1572864 | tf_op jit(solution)/shard_map/psum | solution.py:9
  77.7 1.6 copy-start.11
  79.2 232.6 %all-reduce.6.cloned.1.call-start = ((), (), s32[]{:S(2)}) async-start(), calls=%async_computation.5 | async-start | bytes 1572864 | tf_op jit(solution)/shard_map/psum | solution.py:74
  143.1 103.6 %copy-start.10 = (bf16[128,128]{1,0:T(8,128)(2,1)S(1)}, bf16[128,128]{1,0:T(8,128)(2,1)}, u32[]{:S(2)}) copy-start(bf16[128,128]{1,0:T(8,128)(2,1)} %param.10) | copy-start | bytes 98308
  246.7 177.2 %all-reduce.8.cloned.1.call-start = ((), (), s32[]{:S(2)}) async-start(), calls=%async_computation.7 | async-start | bytes 1572864 | tf_op jit(solution)/shard_map/psum | solution.py:81
  311.9 3.0 copy-start.1
  313.4 3.0 copy-start.2
  317.8 0.9 copy-start.3
  321.3 192.5 %reduce-scatter.2.cloned.1.call-start = ((), (), s32[]{:S(2)}) async-start(), calls=%async_computation.6 | async-start | bytes 1253376 | tf_op jit(solution)/shard_map/reduce_scatter | solution.py:77
  325.5 108.1 %copy-start.7 = (bf16[48,24,128]{0,1,2:T(8,128)(2,1)S(1)}, bf16[48,24,128]{0,1,2:T(8,128)(2,1)}, u32[]{:S(2)}) copy-start(bf16[48,24,128]{0,1,2:T(8,128)(2,1)} %get-tuple-element.17) | copy-start | bytes 884740
  325.6 108.6 %copy-start.8 = (f32[48,24,128]{2,1,0:T(8,128)S(1)}, f32[48,24,128]{2,1,0:T(8,128)}, u32[]{:S(2)}) copy-start(f32[48,24,128]{2,1,0:T(8,128)} %fusion.14) | copy-start | bytes 1769476
  325.6 108.6 %copy-start.9 = (bf16[48,24,128]{2,1,0:T(8,128)(2,1)S(1)}, bf16[48,24,128]{2,1,0:T(8,128)(2,1)}, u32[]{:S(2)}) copy-start(bf16[48,24,128]{2,1,0:T(8,128)(2,1)} %param.7) | copy-start | bytes 884740
  426.4 16.5 %all-to-all-start = ((bf16[24,96,128]{2,0,1:T(8,128)(2,1)}), bf16[24,96,128]{2,0,1:T(8,128)(2,1)S(1)}, u32[]{:S(2)}, u32[]{:S(2)}) async-start(bf16[24,96,128]{2,0,1:T(8,128)(2,1)} %copy.66), calls=%async_computation.1 | async-start | bytes 1179648 | tf_op jit(solution)/shard_map/all_to_all | solution.py:82
  443.1 70.8 %copy-start.5 = (f32[48,6,512]{2,0,1:T(8,128)S(1)}, f32[48,6,512]{2,0,1:T(8,128)}, u32[]{:S(2)}) copy-start(f32[48,6,512]{2,0,1:T(8,128)} %copy-done.4) | copy-start | bytes 1769476
  443.2 86.8 %copy-start.6 = (bf16[48,24,128]{2,1,0:T(8,128)(2,1)S(1)}, bf16[48,24,128]{2,1,0:T(8,128)(2,1)}, u32[]{:S(2)}) copy-start(bf16[48,24,128]{2,1,0:T(8,128)(2,1)} %param.6) | copy-start | bytes 884740
Sparse Core Ops, SparseCore 0:
  14.0 62.2 all-gather.2
  79.9 57.8 all-gather.4
  140.8 102.8 all-reduce.3
  246.8 65.0 all-reduce.5
  321.5 102.3 all-reduce.7
  427.8 86.0 reduce-scatter.1
where the time goes:
time: 540 us; the launch traced here: 539 us
  waiting for transfers between devices  457 us (85%)
  local copies, waits for them, and re-layouts  18.1 us (3%)
  blocking collectives  14.8 us (3%)
  between operations  14.4 us (3%)
  other arithmetic  14.2 us (3%)
  matrix products  13.4 us (2%)
  starting transfers between devices  7.4 us (1%)
    psum x1, waiting for transfers between devices, from_root(): return lax.psum(kept, axis)  100 us
    psum x1, waiting for transfers between devices, shards(): db_total = lax.psum(db_part.astype(jnp.bfloat16), 'row').astype(jnp.float32)  98.3 us
    reduce_scatter x1, waiting for transfers between devices, shards(): lax.psum_scatter(da_part.astype(jnp.bfloat16), 'col', scatter_dimension=1...  70.7 us
    all_gather x1, waiting for transfers between devices, shards(): lax.all_gather(b_sub, 'col', axis=1, tiled=True)  61.6 us
    psum x1, waiting for transfers between devices, shards(): lax.psum(partial_value.astype(jnp.bfloat16), 'depth').astype(jnp.float32)  60 us
    all_gather x1, waiting for transfers between devices, shards(): lax.all_gather(a_sub, 'col', axis=1, tiled=True)  57.4 us
    all_gather x1, blocking collectives, shards(): lax.all_gather(dx_ab.astype(jnp.bfloat16), 'depth', axis=1, tiled=True)  14.8 us
  transfers between devices with their start and end apart: 7, of which 7 were waited for; matrix products, arithmetic and copies ran while one was open for 4% of the time, Pallas kernels for 0%

commit v1 on v0

v1 whole, which is shorter than its diff:
```python
import functools

import jax
import jax.numpy as jnp
from jax import lax
from jax.experimental import pallas as pl
from jax.experimental.pallas import tpu as pltpu
from jax.sharding import PartitionSpec as P

MESH = pl.DeviceIdType.MESH
F32 = jnp.float32
BF16 = jnp.bfloat16
SLOT = 32
LANE = 128
PER = LANE // SLOT


def dot(left, right):
    return jnp.dot(left, right, preferred_element_type=F32)


def norm_rows(values):
    average = jnp.mean(values, axis=0, keepdims=True)
    centered = values - average
    variance = jnp.mean(centered * centered, axis=0, keepdims=True)
    inv_std = lax.rsqrt(variance + 1e-05)
    return (centered * inv_std, inv_std)


def norm_back(x_hat, inv_std, upstream):
    first = jnp.mean(upstream, axis=0, keepdims=True)
    second = jnp.mean(upstream * x_hat, axis=0, keepdims=True)
    return inv_std * (upstream - first - x_hat * second)


def lanes(x, v):
    return x[..., v * LANE : (v + 1) * LANE]


def to_matrix(tiles, slot):
    out = []
    for x in tiles:
        groups, rows = x.shape[0] // PER, x.shape[1]
        x = x.reshape(groups, PER, rows, LANE)
        for s in range(PER):
            acc = None
            for c in range(PER):
                y = x[:, c]
                if c != s:
                    y = pltpu.roll(y, (SLOT * (c - s)) % LANE, 2)
                acc = y if acc is None else jnp.where(slot == c, y, acc)
            out.append(jnp.concatenate([acc[g] for g in range(groups)], axis=-1))
    return out


def from_matrix(matrix, slot):
    count, rows, width = matrix.shape
    x = matrix.reshape(count // PER, PER, rows, width)
    out = []
    for g in range(width // LANE):
        part = lanes(x, g)
        for c in range(PER):
            acc = None
            for s in range(PER):
                y = part[:, s]
                if c != s:
                    y = pltpu.roll(y, (SLOT * (s - c)) % LANE, 2)
                acc = y if acc is None else jnp.where(slot == s, y, acc)
            out.append(acc)
    return out


def kernel(
    dims,
    mask, pair, cot, w_in, w_gate, w_out,
    update_out, grad_out,
    pad, proj, s1, r1, f1, s2, r2, bq, rb, bf, s3, r3, s4, r4, s5, r5, f5, s6, r6,
    gf, s7, r7, s8, r8, f8, s9, r9, su, ru, sg, rg,
    row_send, row_recv, col_send, col_recv, depth_send, depth_recv,
):
    n_d, n_r, n_c, i_block, k_block, ch, hid = dims
    i_q = i_block // n_d
    width = i_q * SLOT
    vl = width // LANE
    hr = hid // n_r
    me_d, me_r, me_c = lax.axis_index("depth"), lax.axis_index("row"), lax.axis_index("col")
    axes = {
        "row": (n_r, me_r, row_send, row_recv),
        "col": (n_c, me_c, col_send, col_recv),
        "depth": (n_d, me_d, depth_send, depth_recv),
    }

    barrier = pltpu.get_barrier_semaphore()
    for axis, (size, me, _, _) in axes.items():
        for o in range(1, size):
            pl.semaphore_signal(barrier, inc=1, device_id={axis: lax.rem(me + o, size)}, device_id_type=MESH)

    def copies(axis, phase, src_at, dst_at):
        size, me, send, recv = axes[axis]
        out = []
        for o in range(1, size):
            to = lax.rem(me + o, size)
            out.append((
                pltpu.make_async_remote_copy(
                    src_ref=src_at(to), dst_ref=dst_at(me), send_sem=send.at[phase, o], recv_sem=recv.at[phase, o],
                    device_id={axis: to}, device_id_type=MESH,
                ),
                pltpu.make_async_remote_copy(
                    src_ref=src_at(to), dst_ref=dst_at(lax.rem(me - o + size, size)), send_sem=send.at[phase, o],
                    recv_sem=recv.at[phase, o], device_id={axis: to}, device_id_type=MESH,
                ),
            ))
        return out

    started = []

    def start(axis, phase, src_at, dst_at):
        both = copies(axis, phase, src_at, dst_at)
        for go, _ in both:
            go.start()
        started.extend(both)
        return both

    def arrive(both):
        for _, come in both:
            come.wait_recv()

    slot = lax.broadcasted_iota(jnp.int32, (1, 1, LANE), 2) // SLOT

    def padded_t(ref):
        pad[:, :k_block, :] = ref[pl.ds(me_d * i_q, i_q)].astype(F32)
        pad[:, k_block:, :] = jnp.zeros((i_q, SLOT - k_block, ch), F32)
        return pad[...].reshape(width, ch).T

    x_hat, inv_std = norm_rows(padded_t(pair))
    normed = x_hat.astype(BF16)
    lane_id = lax.broadcasted_iota(jnp.int32, (1, width), 1)
    row_mask = jnp.zeros((1, width), F32)
    for i in range(i_q):
        here = mask[me_r * i_block + me_d * i_q + i].astype(F32)
        row_mask = jnp.where(lane_id // SLOT == i, here, row_mask)
    col_mask = jnp.zeros((1, width), F32)
    for t in range(k_block):
        here = mask[me_c * k_block + t].astype(F32)
        col_mask = jnp.where(lane_id % SLOT == t, here, col_mask)
    pair_mask = row_mask * col_mask
    w_in_t = w_in[...].astype(F32).T.astype(BF16)
    for block in range(2):
        both = dot(w_in_t[2 * block * hid : 2 * (block + 1) * hid], normed)
        sig, val = jax.nn.sigmoid(both[:hid]), both[hid:]
        proj[2 * block] = sig
        proj[2 * block + 1] = val
        s1[:, block * hr : (block + 1) * hr, :] = (pair_mask * sig * val).astype(BF16).reshape(n_r, hr, width)

    pl.semaphore_wait(barrier, (n_r - 1) + (n_c - 1) + (n_d - 1))
    move = start("row", 0, lambda t: s1.at[t], lambda t: r1.at[t])
    r1[me_r] = s1[me_r]
    cot_t = padded_t(cot)
    gate_val = jax.nn.sigmoid(dot(w_gate[...].astype(F32).T.astype(BF16), normed))
    w_out_t = w_out[...].astype(F32).T.astype(BF16)
    bf[...] = jnp.zeros_like(bf)
    arrive(move)

    x = r1[...].astype(F32)
    for v in range(vl):
        f1[v] = lanes(x, v).reshape(n_r * 2 * hr, LANE)
    for h in range(hr):
        for v in range(vl):
            a_rows = f1[v, pl.ds(h, n_r, stride=2 * hr), :]
            b_rows = f1[v, pl.ds(hr + h, n_r, stride=2 * hr), :]
            s2[h, :, v * LANE : (v + 1) * LANE] = jnp.concatenate([a_rows, b_rows], axis=0).astype(BF16)
    move = start("col", 0, lambda t: s2.at[t], lambda t: r2.at[t])
    r2[me_c] = s2[me_c]
    arrive(move)

    x = r2[...].astype(F32)
    ab = to_matrix([lanes(x, v) for v in range(vl)], slot)
    bq[...] = jnp.concatenate([m[n_r:] for m in ab], axis=0).astype(BF16)
    move = start("depth", 0, lambda t: bq, lambda t: rb.at[t])
    rb[me_d] = bq[...]
    a_mat = jnp.concatenate([m[:n_r] for m in ab], axis=0).astype(BF16)
    arrive(move)

    per_row = i_block // k_block
    groups = n_c * SLOT // LANE

    def strided(d, i):
        at = d * i_q + i
        return pl.ds(SLOT * (at // k_block) + at % k_block, n_r, stride=SLOT * per_row)

    for d in range(n_d):
        x = rb[d].astype(F32)
        for i in range(i_q):
            for g in range(groups):
                bf[g, strided(d, i), :] = lanes(x[i * n_r : (i + 1) * n_r], g)
    b_mat = jnp.concatenate([bf[g].astype(BF16) for g in range(groups)], axis=-1)
    tri = lax.dot_general(a_mat, b_mat, (((1,), (1,)), ((), ())), preferred_element_type=F32)

    for c, x in enumerate(from_matrix(tri.reshape(i_q, n_r, n_c * SLOT), slot)):
        s3[c] = x.reshape(vl * n_r, LANE)
    size3 = vl * n_r

    def part3(ref):
        return lambda t: ref.at[pl.ds(pl.multiple_of(t * size3, size3), size3)]

    move = start("col", 1, lambda t: s3.at[t], part3(r3))
    r3[pl.ds(pl.multiple_of(me_c * size3, size3), size3), :] = s3[me_c]
    arrive(move)
    for r in range(n_r):
        for v in range(vl):
            s4[r, :, v * LANE : (v + 1) * LANE] = r3[pl.ds(v * n_r + r, n_c, stride=size3), :].astype(BF16)
    move = start("row", 1, lambda t: s4.at[t], lambda t: r4.at[t])
    r4[me_r] = s4[me_r]
    arrive(move)

    y_hat, tri_std = norm_rows(r4[...].astype(F32).reshape(hid, width))
    out_proj = dot(w_out_t, y_hat.astype(BF16))
    d_o = (cot_t * gate_val).astype(BF16)
    d_y = dot(w_out[...], d_o)
    tri_grad = norm_back(y_hat, tri_std, d_y)
    s5[...] = tri_grad.astype(BF16).reshape(n_r, hr, width)
    move = start("row", 2, lambda t: s5.at[t], lambda t: r5.at[t])
    r5[me_r] = s5[me_r]

    def natural(x):
        return x.T.reshape(i_q, SLOT, ch)[:, :k_block, :].reshape(i_q * k_block, ch).astype(BF16)

    su[...] = natural(gate_val * out_proj)
    update_move = start("depth", 1, lambda t: su, lambda t: ru.at[t])
    ru[me_d] = su[...]
    d_gate_pre = (cot_t * out_proj * gate_val * (1.0 - gate_val)).astype(BF16)
    d_gate = dot(w_gate[...], d_gate_pre)
    arrive(move)

    x = r5[...].astype(F32)
    for v in range(vl):
        f5[v] = lanes(x, v).reshape(n_r * hr, LANE)
    for h in range(hr):
        for v in range(vl):
            s6[h, v * n_r : (v + 1) * n_r, :] = f5[v, pl.ds(h, n_r, stride=hr), :]
    move = start("col", 2, lambda t: s6.at[t], lambda t: r6.at[t])
    r6[me_c] = s6[me_c]
    arrive(move)
    tg = jnp.concatenate(to_matrix([r6[:, v * n_r : (v + 1) * n_r, :] for v in range(vl)], slot), axis=0)
    tg_t = tg.T.astype(BF16)
    part_b = dot(tg_t, a_mat)
    for g in range(groups):
        gf[g] = lanes(part_b, g)
    for d in range(n_d):
        s7[d] = jnp.concatenate(
            [
                jnp.concatenate([gf[g, strided(d, i), :] for g in range(groups)], axis=-1)
                for i in range(i_q)
            ],
            axis=0,
        ).astype(BF16)
    move = start("depth", 2, lambda t: s7.at[t], lambda t: r7.at[t])
    r7[me_d] = s7[me_d]
    grad_a = dot(tg.astype(BF16), b_mat)
    arrive(move)
    grad_b = r7[0].astype(F32)
    for d in range(1, n_d):
        grad_b = grad_b + r7[d].astype(F32)

    both = jnp.concatenate(
        [grad_a.reshape(i_q, n_r, n_c * SLOT), grad_b.reshape(i_q, n_r, n_c * SLOT)], axis=1
    )
    for c, x in enumerate(from_matrix(both, slot)):
        for v in range(vl):
            s8[c, :, v * LANE : (v + 1) * LANE] = x[v].astype(BF16)
    move = start("col", 3, lambda t: s8.at[t], lambda t: r8.at[t])
    r8[me_c] = s8[me_c]
    arrive(move)
    x = r8[...].astype(F32)
    for v in range(vl):
        f8[v] = lanes(x, v).reshape(n_c * 2 * n_r, LANE)
    for r in range(n_r):
        for v in range(vl):
            for block in range(2):
                s9[r, block * hr : (block + 1) * hr, v * LANE : (v + 1) * LANE] = f8[
                    v, pl.ds(block * n_r + r, n_c, stride=2 * n_r), :
                ].astype(BF16)
    move = start("row", 3, lambda t: s9.at[t], lambda t: r9.at[t])
    r9[me_r] = s9[me_r]
    arrive(move)

    d_normed = d_gate
    for block in range(2):
        grad = r9[:, block * hr : (block + 1) * hr, :].astype(F32).reshape(hid, width) * pair_mask
        sig, val = proj[2 * block], proj[2 * block + 1]
        d_pre = (grad * val * sig * (1.0 - sig)).astype(BF16)
        d_val = (grad * sig).astype(BF16)
        d_normed = d_normed + dot(w_in[:, 2 * block * hid : (2 * block + 1) * hid], d_pre)
        d_normed = d_normed + dot(w_in[:, (2 * block + 1) * hid : (2 * block + 2) * hid], d_val)
    sg[...] = natural(norm_back(x_hat, inv_std, d_normed))
    move = start("depth", 3, lambda t: sg, lambda t: rg.at[t])
    rg[me_d] = sg[...]
    arrive(update_move)
    for d in range(n_d):
        update_out[d * i_q : (d + 1) * i_q] = ru[d].astype(F32).reshape(i_q, k_block, ch).astype(BF16)
    arrive(move)
    for d in range(n_d):
        grad_out[d * i_q : (d + 1) * i_q] = rg[d].astype(F32).reshape(i_q, k_block, ch).astype(BF16)
    for go, _ in started:
        go.wait_send()


def shards(sizes, pair, cotangent, w_in, w_gate, w_out, residue_mask):
    n_d, n_r, n_c = sizes
    i_block, k_block, ch = pair.shape
    hid = w_out.shape[0]
    i_q = i_block // n_d
    width = i_q * SLOT
    vl = width // LANE
    hr = hid // n_r
    groups = n_c * SLOT // LANE
    rows_q = i_q * n_r
    full = n_c * SLOT
    vm = pltpu.VMEM
    scratch = [
        vm((i_q, SLOT, ch), F32),
        vm((4, hid, width), F32),
        vm((n_r, 2 * hr, width), BF16),
        vm((n_r, 2 * hr, width), BF16),
        vm((vl, n_r * 2 * hr, LANE), F32),
        vm((n_c, 2 * n_r, width), BF16),
        vm((n_c, 2 * n_r, width), BF16),
        vm((rows_q, full), BF16),
        vm((n_d, rows_q, full), BF16),
        vm((groups, full, LANE), F32),
        vm((n_c, vl * n_r, LANE), F32),
        vm((n_c * vl * n_r, LANE), F32),
        vm((n_r, hr, width), BF16),
        vm((n_r, hr, width), BF16),
        vm((n_r, hr, width), BF16),
        vm((n_r, hr, width), BF16),
        vm((vl, n_r * hr, LANE), F32),
        vm((n_c, vl * n_r, LANE), F32),
        vm((n_c, vl * n_r, LANE), F32),
        vm((groups, full, LANE), F32),
        vm((n_d, rows_q, full), BF16),
        vm((n_d, rows_q, full), BF16),
        vm((n_c, 2 * n_r, width), BF16),
        vm((n_c, 2 * n_r, width), BF16),
        vm((vl, n_c * 2 * n_r, LANE), F32),
        vm((n_r, 2 * hr, width), BF16),
        vm((n_r, 2 * hr, width), BF16),
        vm((i_q * k_block, ch), BF16),
        vm((n_d, i_q * k_block, ch), BF16),
        vm((i_q * k_block, ch), BF16),
        vm((n_d, i_q * k_block, ch), BF16),
    ]
    for size in (n_r, n_c, n_d):
        scratch += [pltpu.SemaphoreType.DMA((4, size))] * 2
    whole = pl.BlockSpec(memory_space=pltpu.VMEM)
    return pl.pallas_call(
        functools.partial(kernel, (n_d, n_r, n_c, i_block, k_block, ch, hid)),
        out_shape=(jax.ShapeDtypeStruct(pair.shape, BF16),) * 2,
        in_specs=[pl.BlockSpec(memory_space=pltpu.SMEM)] + [whole] * 5,
        out_specs=(whole, whole),
        scratch_shapes=scratch,
        compiler_params=pltpu.CompilerParams(
            collective_id=0, has_side_effects=True, vmem_limit_bytes=40 * 1024 * 1024
        ),
    )(residue_mask, pair, cotangent, w_in, w_gate, w_out)


def solution(mesh):
    in_specs = (P("row", "col", None), P("row", "col", None), P(), P(), P(), P())
    out_specs = (P("row", "col", None), P("row", "col", None))
    sizes = (mesh.shape["depth"], mesh.shape["row"], mesh.shape["col"])
    return jax.shard_map(
        functools.partial(shards, sizes), mesh=mesh, in_specs=in_specs, out_specs=out_specs, check_vma=False
    )
```

time: 540 us -> 117 us (0.22)
  the two profiles are of different devices: /device:TPU:24 before, /device:TPU:1 now
where the time goes in v1:
time: 117 us
  Pallas kernels  110 us (94%)
  local copies, waits for them, and re-layouts  6.44 us (6%)
    pallas_call x1, Pallas kernels, shards(): pl.pallas_call(functools.partial(kernel, (n_d, n_r, n_c, i_block, k_block...  110 us
    unnamed x14, local copies, waits for them, and re-layouts  6.44 us

profile of v1, /device:TPU:1, one launch (start us, length us, event | category | flops | bytes accessed | tf_op | source)
XLA Modules:
  0.0 117.1 jit_solution(5106076317904464409)
XLA Ops:
  0.6 0.0 copy-start
  0.6 1.0 copy-done
  1.6 0.0 copy-start.1
  1.6 1.0 copy-done.1
  2.6 0.0 copy-start.2
  2.6 0.9 copy-done.2
  3.5 0.0 copy-start.3
  3.5 0.8 copy-done.3
  4.2 0.0 copy-start.4
  4.2 0.8 copy-done.4
  5.0 0.0 copy-start.5
  5.0 0.7 copy-done.5
  5.7 110.0 %shard_map.77 = (bf16[48,24,128]{2,1,0:T(8,128)(2,1)S(1)}, bf16[48,24,128]{2,1,0:T(8,128)(2,1)S(1)}) custom-call(s32[384]{0:T(512)S(1)} %copy-done.5, bf16[48,24,128]{2,1,0:T(8,128)(2,1)S(1)} %copy-done, bf16[48,24,128]{2,1,0:T(8,128)(2,1)S(1)} %copy-done.1, bf16[128,512]{1,0:T(8,128)(2,1)S(1)} %copy-done.2, bf16[128,128]{1,0:T(8,128)(2,1)S(1)} %copy-done.3, ...), custom_call_target="tpu_custom_call" | custom-call | tf_op jit(solution)/shard_map/pallas_call | solution.py:356
  115.7 0.7 copy.10
  116.4 0.7 copy.11
Async XLA Ops:
  0.6 1.0 copy-start
  1.6 1.0 copy-start.1
  2.6 0.9 copy-start.2
  3.5 0.8 copy-start.3
  4.2 0.8 copy-start.4
  5.0 0.7 copy-start.5

commit v2 on v1

v2 whole, which is shorter than its diff:
```python
import functools

import jax
import jax.numpy as jnp
from jax import lax
from jax.experimental import pallas as pl
from jax.experimental.pallas import tpu as pltpu
from jax.sharding import PartitionSpec as P

MESH = pl.DeviceIdType.MESH
F32 = jnp.float32
BF16 = jnp.bfloat16
SLOT = 32
LANE = 128
PER = LANE // SLOT


def dot(left, right):
    return jnp.dot(left, right, preferred_element_type=F32)


def norm_rows(values):
    average = jnp.mean(values, axis=0, keepdims=True)
    centered = values - average
    variance = jnp.mean(centered * centered, axis=0, keepdims=True)
    inv_std = lax.rsqrt(variance + 1e-05)
    return (centered * inv_std, inv_std)


def norm_back(x_hat, inv_std, upstream):
    first = jnp.mean(upstream, axis=0, keepdims=True)
    second = jnp.mean(upstream * x_hat, axis=0, keepdims=True)
    return inv_std * (upstream - first - x_hat * second)


def lanes(x, v):
    return x[..., v * LANE : (v + 1) * LANE]


def to_matrix(tiles, slot):
    out = []
    for x in tiles:
        groups, rows = x.shape[0] // PER, x.shape[1]
        x = x.reshape(groups, PER, rows, LANE)
        for s in range(PER):
            acc = None
            for c in range(PER):
                y = x[:, c]
                if c != s:
                    y = pltpu.roll(y, (SLOT * (c - s)) % LANE, 2)
                acc = y if acc is None else jnp.where(slot == c, y, acc)
            out.append(jnp.concatenate([acc[g] for g in range(groups)], axis=-1))
    return out


def from_matrix(matrix, slot):
    count, rows, width = matrix.shape
    x = matrix.reshape(count // PER, PER, rows, width)
    out = []
    for g in range(width // LANE):
        part = lanes(x, g)
        for c in range(PER):
            acc = None
            for s in range(PER):
                y = part[:, s]
                if c != s:
                    y = pltpu.roll(y, (SLOT * (s - c)) % LANE, 2)
                acc = y if acc is None else jnp.where(slot == s, y, acc)
            out.append(acc)
    return out


def kernel(
    dims,
    mask_hbm, pair_hbm, cot_hbm, w_in_hbm, w_gate_hbm, w_out_hbm,
    update_out, grad_out,
    mask, pair, cot, w_in, w_gate, w_out, in_sem,
    pad, proj, s1, r1, f1, s2, r2, bn, s3, r3, s4, r4, s5, r5, f5, s6, r6, tgf,
    gf, s8, r8, f8, s9, r9, su, ru, sg, rg,
    z_send, z_recv, col_send, col_recv, depth_send, depth_recv,
):
    n_d, n_r, n_c, n_x, i_block, k_block, ch, hid = dims
    n_zh, n_dd, n_y = n_r // 2, n_d // 2, n_c // n_x
    n_z = n_zh * n_d
    hz = hid // n_z
    i_q = i_block // n_d
    width = i_q * SLOT
    vl = width // LANE
    half = 2 * n_zh
    full = n_c * SLOT
    groups = full // LANE
    me_d, me_r, me_c = lax.axis_index("depth"), lax.axis_index("row"), lax.axis_index("col")
    me_zh, me_core = me_r // 2, me_r % 2

    def z_slot(zh, d):
        return (d % n_dd) * half + (d // n_dd) * n_zh + zh

    def c_slot(c):
        return ((c // 2) % 2) * half + (c % 2) * n_zh + c // 4

    me_s, me_p = z_slot(me_zh, me_d), c_slot(me_c)
    me_dd = me_p % 2

    def z_peer(o):
        z = lax.rem(me_zh * n_d + me_d + o + n_z, n_z)
        zh, d = z // n_d, z % n_d
        return {"row": zh * 2 + me_core, "depth": d}, z_slot(zh, d)

    def c_peer(core, ox, oy):
        x = lax.rem(me_c // n_y + ox + n_x, n_x)
        y = lax.rem(me_c % n_y + oy + n_y, n_y)
        c = x * n_y + y
        return {"row": me_zh * 2 + core, "col": c}, c_slot(c)

    def d_peer(o):
        d = lax.rem(me_d + o + n_d, n_d)
        return {"depth": d}, d

    z_offsets = sorted(range(1, n_z), key=lambda o: -min(o, n_z - o))
    c_offsets = sorted(
        [(x, y) for x in range(n_x) for y in range(n_y)],
        key=lambda o: -(min(o[0], n_x - o[0]) + min(o[1], n_y - o[1])),
    )
    d_offsets = list(range(1, n_d))

    z_list = [z_peer(o) + (z_peer(-o)[1], k) for k, o in enumerate(z_offsets)]
    d_list = [d_peer(o) + (d_peer(-o)[1], k) for k, o in enumerate(d_offsets)]
    c_same, c_other = [], []
    for k, (ox, oy) in enumerate(c_offsets):
        if (ox, oy) != (0, 0):
            c_same.append(c_peer(me_core, ox, oy) + (c_peer(me_core, -ox, -oy)[1], k))
        c_other.append(c_peer(1 - me_core, ox, oy) + (c_peer(me_core, -ox, -oy)[1], n_c + k))

    barrier = pltpu.get_barrier_semaphore()
    peers = z_list + c_same + c_other
    for to, _, _, _ in peers:
        pl.semaphore_signal(barrier, inc=1, device_id=to, device_id_type=MESH)

    own_rows = pl.ds(me_d * i_q, i_q)
    fetch = [
        pltpu.make_async_copy(a, b, in_sem.at[k])
        for k, (a, b) in enumerate([
            (pair_hbm.at[own_rows], pair), (w_in_hbm, w_in), (mask_hbm, mask),
            (cot_hbm.at[own_rows], cot), (w_gate_hbm, w_gate), (w_out_hbm, w_out),
        ])
    ]
    for f in fetch:
        f.start()

    started = []

    def start(peer_list, send, recv, src_at, dst_mine, dst_from):
        both = []
        for to, slot_to, slot_from, k in peer_list:
            go = pltpu.make_async_remote_copy(
                src_ref=src_at(slot_to), dst_ref=dst_mine, send_sem=send.at[k], recv_sem=recv.at[k],
                device_id=to, device_id_type=MESH,
            )
            come = pltpu.make_async_remote_copy(
                src_ref=src_at(slot_to), dst_ref=dst_from(slot_from), send_sem=send.at[k], recv_sem=recv.at[k],
                device_id=to, device_id_type=MESH,
            )
            go.start()
            both.append((go, come))
        started.extend(both)
        return both

    def arrive(both):
        for _, come in both:
            come.wait_recv()

    def start_z(phase, s, r):
        both = start(z_list, z_send.at[phase], z_recv.at[phase], lambda t: s.at[t], r.at[me_s], lambda t: r.at[t])
        r[me_s] = s[me_s]
        return both

    def start_c(phase, s, r):
        both = start(c_same, col_send.at[phase], col_recv.at[phase], lambda t: s.at[t], r.at[me_p], lambda t: r.at[t])
        r[me_p] = s[me_p]
        return both

    def start_cc(phase, s, r):
        sems = (col_send.at[phase], col_recv.at[phase])
        both = start(c_same, *sems, lambda t: s.at[t], r.at[me_core, me_p], lambda t: r.at[me_core, t])
        both += start(c_other, *sems, lambda t: s.at[t], r.at[me_core, me_p], lambda t: r.at[1 - me_core, t])
        r[me_core, me_p] = s[me_p]
        return both

    def start_d(phase, s, r):
        both = start(d_list, depth_send.at[phase], depth_recv.at[phase], lambda t: s, r.at[me_d], lambda t: r.at[t])
        r[me_d] = s[...]
        return both

    slot = lax.broadcasted_iota(jnp.int32, (1, 1, LANE), 2) // SLOT

    def padded_t(ref):
        pad[:, :k_block, :] = ref[...].astype(F32)
        pad[:, k_block:, :] = jnp.zeros((i_q, SLOT - k_block, ch), F32)
        return pad[...].reshape(width, ch).T

    def pack(x):
        parts = [lanes(x, v).reshape(n_z, hz, LANE) for v in range(vl)]
        short = s5.shape[1] - vl * hz
        if short:
            parts.append(jnp.zeros((n_z, short, LANE), F32))
        return jnp.concatenate(parts, axis=1).astype(BF16)

    fetch[0].wait()
    x_hat, inv_std = norm_rows(padded_t(pair))
    normed = x_hat.astype(BF16)
    fetch[1].wait()
    w_in_t = w_in[...].astype(F32).T.astype(BF16)
    fetch[2].wait()
    lane_id = lax.broadcasted_iota(jnp.int32, (1, width), 1)
    row_mask = jnp.zeros((1, width), F32)
    for i in range(i_q):
        here = mask[me_r * i_block + me_d * i_q + i].astype(F32)
        row_mask = jnp.where(lane_id // SLOT == i, here, row_mask)
    col_mask = jnp.zeros((1, width), F32)
    for t in range(k_block):
        here = mask[me_c * k_block + t].astype(F32)
        col_mask = jnp.where(lane_id % SLOT == t, here, col_mask)
    pair_mask = row_mask * col_mask
    parts = []
    for block in range(2):
        both = dot(w_in_t[2 * block * hid : 2 * (block + 1) * hid], normed)
        sig, val = jax.nn.sigmoid(both[:hid]), both[hid:]
        proj[2 * block] = sig
        proj[2 * block + 1] = val
        parts.append((pair_mask * sig * val).reshape(n_z, hz, width))
    s1[...] = jnp.concatenate(parts, axis=1).astype(BF16)

    pl.semaphore_wait(barrier, len(peers))
    move = start_z(0, s1, r1)
    for f in fetch[3:]:
        f.wait()
    cot_t = padded_t(cot)
    gate_val = jax.nn.sigmoid(dot(w_gate[...].astype(F32).T.astype(BF16), normed))
    w_out_t = w_out[...].astype(F32).T.astype(BF16)
    arrive(move)

    x = r1[...].astype(F32)
    for v in range(vl):
        f1[v] = lanes(x, v).reshape(n_z * 2 * hz, LANE)
    for h in range(hz):
        for v in range(vl):
            a0, b0, a1, b1 = (
                f1[v, pl.ds(dd * half * 2 * hz + block * hz + h, half, stride=2 * hz), :]
                for dd in range(2) for block in range(2)
            )
            at = slice(v * LANE, (v + 1) * LANE)
            s2[2 * h, :, at] = jnp.concatenate([a0, a1, b0, b1], axis=0).astype(BF16)
            s2[2 * h + 1, :, at] = jnp.concatenate([a1, a0, b0, b1], axis=0).astype(BF16)
    move = start_cc(0, s2, r2)
    arrive(move)

    for core in range(2):
        x = r2[core, :, 2 * half :, :].astype(F32)
        for i, m in enumerate(to_matrix([lanes(x, v) for v in range(vl)], slot)):
            for dd in range(n_dd):
                at = ((core * n_dd + dd) * i_q + i) * half
                for g in range(groups):
                    bn[g, at : at + half, :] = lanes(m[dd * half : (dd + 1) * half], g)
    rows = []
    for core in range(2):
        for q in range(half):
            rows.append(jnp.concatenate(
                [bn[g, pl.ds(core * k_block * half + q, k_block, stride=half), :] for g in range(groups)], axis=-1
            ))
            rows.append(jnp.zeros((SLOT - k_block, full), F32))
    b_mat = jnp.concatenate(rows, axis=0).astype(BF16)
    x = r2[me_core, :, :half, :].astype(F32)
    a_own = jnp.concatenate(to_matrix([lanes(x, v) for v in range(vl)], slot), axis=0).astype(BF16)
    tri = lax.dot_general(a_own, b_mat, (((1,), (1,)), ((), ())), preferred_element_type=F32)
    for c, x in enumerate(from_matrix(tri.reshape(i_q, half, full), slot)):
        s3[c] = x.reshape(vl * half, LANE)
    size3 = vl * half

    def rows3(t):
        return pl.ds(pl.multiple_of(t * size3, size3), size3)

    move = start(
        c_same, col_send.at[1], col_recv.at[1], lambda t: s3.at[t], r3.at[rows3(me_p)], lambda t: r3.at[rows3(t)]
    )
    r3[rows3(me_p), :] = s3[me_p]

    rows = []
    for core in range(2):
        x = r2[core, :, : 2 * half, :].astype(F32)
        rows += to_matrix([lanes(x, v) for v in range(vl)], slot)
    a_mat = jnp.concatenate(rows, axis=0).astype(BF16)
    arrive(move)

    for dd in range(n_dd):
        for q in range(half):
            parts = [r3[pl.ds(dd * size3 + v * half + q, hz, stride=2 * size3), :] for v in range(vl)]
            short = s4.shape[1] - vl * hz
            if short:
                parts.append(jnp.zeros((short, LANE), F32))
            s4[dd * half + q] = jnp.concatenate(parts, axis=0).astype(BF16)
    move = start_z(1, s4, r4)
    arrive(move)

    x = r4[...].astype(F32)
    tri_t = jnp.concatenate([x[:, v * hz : (v + 1) * hz, :].reshape(hid, LANE) for v in range(vl)], axis=-1)
    y_hat, tri_std = norm_rows(tri_t)
    out_proj = dot(w_out_t, y_hat.astype(BF16))
    d_o = (cot_t * gate_val).astype(BF16)
    d_y = dot(w_out[...], d_o)
    s5[...] = pack(norm_back(y_hat, tri_std, d_y))
    move = start_z(2, s5, r5)

    def natural(x):
        return x.T.reshape(i_q, SLOT, ch)[:, :k_block, :].reshape(i_q * k_block, ch).astype(BF16)

    su[...] = natural(gate_val * out_proj)
    update_move = start_d(0, su, ru)
    d_gate_pre = (cot_t * out_proj * gate_val * (1.0 - gate_val)).astype(BF16)
    d_gate = dot(w_gate[...], d_gate_pre)
    arrive(move)

    pitch = s5.shape[1]
    f5[...] = r5[...].astype(F32).reshape(n_z * pitch, LANE)
    for h in range(hz):
        for v in range(vl):
            t0, t1 = (f5[pl.ds(dd * half * pitch + v * hz + h, half, stride=pitch), :] for dd in range(2))
            at = slice(v * LANE, (v + 1) * LANE)
            s6[2 * h, :, at] = jnp.concatenate([t0, t1], axis=0).astype(BF16)
            s6[2 * h + 1, :, at] = jnp.concatenate([t1, t0], axis=0).astype(BF16)
    move = start_cc(2, s6, r6)
    arrive(move)
    for core in range(2):
        x = r6[core].astype(F32)
        for i, m in enumerate(to_matrix([lanes(x, v) for v in range(vl)], slot)):
            tgf[core, i] = m
    tg_own = tgf[me_core, :, :half, :].reshape(i_q * half, full).astype(BF16)
    mine = pl.ds(pl.multiple_of(me_core * (full // 2), full // 2), full // 2)
    tg_t = tgf[:, :, :, mine].reshape(2 * i_q * 2 * half, full // 2).T.astype(BF16)
    part_b = dot(tg_t, a_mat)
    for g in range(groups):
        gf[g] = lanes(part_b, g)
    grad_a = dot(tg_own, b_mat).reshape(i_q, half, full)
    rows = []
    for i in range(i_q):
        rows.append(grad_a[i])
        rows.append(jnp.concatenate(
            [gf[g, pl.ds(me_dd * i_q + i, half, stride=SLOT), :] for g in range(groups)], axis=-1
        ))
    both = jnp.concatenate(rows, axis=0).reshape(i_q, 2 * half, full)
    for c, x in enumerate(from_matrix(both, slot)):
        for v in range(vl):
            s8[c, :, v * LANE : (v + 1) * LANE] = x[v].astype(BF16)
    move = start_c(3, s8, r8)
    arrive(move)
    x = r8[...].astype(F32)
    for v in range(vl):
        f8[v] = lanes(x, v).reshape(n_c * 2 * half, LANE)
    for dd in range(n_dd):
        for q in range(half):
            for v in range(vl):
                s9[dd * half + q, :, v * LANE : (v + 1) * LANE] = jnp.concatenate(
                    [
                        f8[v, pl.ds((dd * 2 + block) * half + q, hz, stride=4 * half), :]
                        for block in range(2)
                    ],
                    axis=0,
                ).astype(BF16)
    move = start_z(3, s9, r9)
    arrive(move)

    d_normed = d_gate
    x = r9[...].astype(F32)
    for block in range(2):
        grad = x[:, block * hz : (block + 1) * hz, :].reshape(hid, width) * pair_mask
        sig, val = proj[2 * block], proj[2 * block + 1]
        d_pre = (grad * val * sig * (1.0 - sig)).astype(BF16)
        d_val = (grad * sig).astype(BF16)
        d_normed = d_normed + dot(w_in[:, 2 * block * hid : (2 * block + 1) * hid], d_pre)
        d_normed = d_normed + dot(w_in[:, (2 * block + 1) * hid : (2 * block + 2) * hid], d_val)
    sg[...] = natural(norm_back(x_hat, inv_std, d_normed))
    move = start_d(1, sg, rg)
    arrive(update_move)
    for d in range(n_d):
        update_out[d * i_q : (d + 1) * i_q] = ru[d].astype(F32).reshape(i_q, k_block, ch).astype(BF16)
    arrive(move)
    for d in range(n_d):
        grad_out[d * i_q : (d + 1) * i_q] = rg[d].astype(F32).reshape(i_q, k_block, ch).astype(BF16)
    for go, _ in started:
        go.wait_send()


def shards(sizes, pair, cotangent, w_in, w_gate, w_out, residue_mask):
    n_d, n_r, n_c = sizes
    n_x = 4 if n_c == 16 else 2
    i_block, k_block, ch = pair.shape
    hid = w_out.shape[0]
    i_q = i_block // n_d
    width = i_q * SLOT
    vl = width // LANE
    n_z = (n_r // 2) * n_d
    half = n_r
    hz = hid // n_z
    full = n_c * SLOT
    groups = max(full // LANE, 1)
    pitch = -(-vl * hz // 16) * 16
    vm = pltpu.VMEM
    scratch = [
        pltpu.SMEM(residue_mask.shape, jnp.int32),
        vm((i_q, k_block, ch), BF16),
        vm((i_q, k_block, ch), BF16),
        vm(w_in.shape, BF16),
        vm(w_gate.shape, BF16),
        vm(w_out.shape, BF16),
        pltpu.SemaphoreType.DMA((6,)),
        vm((i_q, SLOT, ch), F32),
        vm((4, hid, width), F32),
        vm((n_z, 2 * hz, width), BF16),
        vm((n_z, 2 * hz, width), BF16),
        vm((vl, n_z * 2 * hz, LANE), F32),
        vm((n_c, 4 * half, width), BF16),
        vm((2, n_c, 4 * half, width), BF16),
        vm((groups, 2 * k_block * half, LANE), F32),
        vm((n_c, vl * half, LANE), F32),
        vm((n_c * vl * half, LANE), F32),
        vm((n_z, pitch, LANE), BF16),
        vm((n_z, pitch, LANE), BF16),
        vm((n_z, pitch, LANE), BF16),
        vm((n_z, pitch, LANE), BF16),
        vm((n_z * pitch, LANE), F32),
        vm((n_c, 2 * half, width), BF16),
        vm((2, n_c, 2 * half, width), BF16),
        vm((2, i_q, 2 * half, full), F32),
        vm((groups, full // 2, LANE), F32),
        vm((n_c, 2 * half, width), BF16),
        vm((n_c, 2 * half, width), BF16),
        vm((vl, n_c * 2 * half, LANE), F32),
        vm((n_z, 2 * hz, width), BF16),
        vm((n_z, 2 * hz, width), BF16),
        vm((i_q * k_block, ch), BF16),
        vm((n_d, i_q * k_block, ch), BF16),
        vm((i_q * k_block, ch), BF16),
        vm((n_d, i_q * k_block, ch), BF16),
    ]
    for phases, size in ((4, n_z), (4, 2 * n_c), (2, n_d)):
        scratch += [pltpu.SemaphoreType.DMA((phases, size))] * 2
    whole = pl.BlockSpec(memory_space=pltpu.VMEM)
    return pl.pallas_call(
        functools.partial(kernel, (n_d, n_r, n_c, n_x, i_block, k_block, ch, hid)),
        out_shape=(jax.ShapeDtypeStruct(pair.shape, BF16),) * 2,
        in_specs=[pl.BlockSpec(memory_space=pl.ANY)] * 6,
        out_specs=(whole, whole),
        scratch_shapes=scratch,
        compiler_params=pltpu.CompilerParams(
            collective_id=0, has_side_effects=True, vmem_limit_bytes=60 * 1024 * 1024
        ),
    )(residue_mask, pair, cotangent, w_in, w_gate, w_out)


def solution(mesh):
    in_specs = (P("row", "col", None), P("row", "col", None), P(), P(), P(), P())
    out_specs = (P("row", "col", None), P("row", "col", None))
    sizes = (mesh.shape["depth"], mesh.shape["row"], mesh.shape["col"])
    return jax.shard_map(
        functools.partial(shards, sizes), mesh=mesh, in_specs=in_specs, out_specs=out_specs, check_vma=False
    )
```

time: 117 us -> 101 us (0.86)
  the two profiles are of different devices: /device:TPU:1 before, /device:TPU:24 now
where the time goes in v2:
time: 101 us
  Pallas kernels  97.5 us (97%)
  local copies, waits for them, and re-layouts  2.47 us (2%)
    pallas_call x1, Pallas kernels, shards(): pl.pallas_call(functools.partial(kernel, (n_d, n_r, n_c, n_x, i_block, k_...  97.5 us
    unnamed x4, local copies, waits for them, and re-layouts  2.47 us

profile of v2, /device:TPU:24, one launch (start us, length us, event | category | flops | bytes accessed | tf_op | source)
XLA Modules:
  0.0 100.6 jit_solution(7976755842379141553)
XLA Ops:
  0.6 97.5 %shard_map.77 = (bf16[48,24,128]{2,1,0:T(8,128)(2,1)}, bf16[48,24,128]{2,1,0:T(8,128)(2,1)}) custom-call(s32[384]{0:T(512)} %mask_hbm.1, bf16[48,24,128]{2,1,0:T(8,128)(2,1)} %pair_hbm.1, bf16[48,24,128]{2,1,0:T(8,128)(2,1)} %cot_hbm.1, bf16[128,512]{1,0:T(8,128)(2,1)} %w_in_hbm.1, bf16[128,128]{1,0:T(8,128)(2,1)} %w_gate_hbm.1, bf16[128,128]{1,0:T(8,128)(2,1)} %w_out_hbm.1), custom_call_target="tpu_custom_call" | custom-call | tf_op jit(solution)/shard_map/pallas_call | solution.py:447
  98.1 0.0 copy-start
  98.1 1.7 %copy.10 = bf16[48,24,128]{2,1,0:T(8,128)(2,1)} copy(bf16[48,24,128]{2,1,0:T(8,128)(2,1)} %get-tuple-element.4) | data formatting | bytes 589824
  99.9 0.0 copy-done
  99.9 0.7 copy.11
Async XLA Ops:
  98.1 1.8 %copy-start = (bf16[48,24,128]{2,1,0:T(8,128)(2,1)S(1)}, bf16[48,24,128]{2,1,0:T(8,128)(2,1)}, u32[]{:S(2)}) copy-start(bf16[48,24,128]{2,1,0:T(8,128)(2,1)} %get-tuple-element.5) | copy-start | bytes 884740

commit v3 on v2

--- a/solution.py
+++ b/solution.py
@@ -75,9 +75,9 @@
     mask_hbm, pair_hbm, cot_hbm, w_in_hbm, w_gate_hbm, w_out_hbm,
     update_out, grad_out,
     mask, pair, cot, w_in, w_gate, w_out, in_sem,
-    pad, proj, s1, r1, f1, s2, r2, bn, s3, r3, s4, r4, s5, r5, f5, s6, r6, tgf,
+    pad, proj, s1, r1, f1, s2a, s2b, r2a, r2b, bn, s3, r3, s4, r4, s5, r5, f5, s6, r6, tgf,
     gf, s8, r8, f8, s9, r9, su, ru, sg, rg,
-    z_send, z_recv, col_send, col_recv, depth_send, depth_recv,
+    z_send, z_recv, col_send, col_recv, depth_send, depth_recv, twin_send, twin_recv,
 ):
     n_d, n_r, n_c, n_x, i_block, k_block, ch, hid = dims
     n_zh, n_dd, n_y = n_r // 2, n_d // 2, n_c // n_x
@@ -106,11 +106,11 @@
         zh, d = z // n_d, z % n_d
         return {"row": zh * 2 + me_core, "depth": d}, z_slot(zh, d)
 
-    def c_peer(core, ox, oy):
+    def c_peer(ox, oy):
         x = lax.rem(me_c // n_y + ox + n_x, n_x)
         y = lax.rem(me_c % n_y + oy + n_y, n_y)
         c = x * n_y + y
-        return {"row": me_zh * 2 + core, "col": c}, c_slot(c)
+        return {"col": c}, c_slot(c)
 
     def d_peer(o):
         d = lax.rem(me_d + o + n_d, n_d)
@@ -125,15 +125,14 @@
 
     z_list = [z_peer(o) + (z_peer(-o)[1], k) for k, o in enumerate(z_offsets)]
     d_list = [d_peer(o) + (d_peer(-o)[1], k) for k, o in enumerate(d_offsets)]
-    c_same, c_other = [], []
-    for k, (ox, oy) in enumerate(c_offsets):
-        if (ox, oy) != (0, 0):
-            c_same.append(c_peer(me_core, ox, oy) + (c_peer(me_core, -ox, -oy)[1], k))
-        c_other.append(c_peer(1 - me_core, ox, oy) + (c_peer(me_core, -ox, -oy)[1], n_c + k))
+    c_list = [
+        c_peer(ox, oy) + (c_peer(-ox, -oy)[1], k) for k, (ox, oy) in enumerate(c_offsets) if (ox, oy) != (0, 0)
+    ]
+    twin = {"row": me_zh * 2 + 1 - me_core}
 
     barrier = pltpu.get_barrier_semaphore()
-    peers = z_list + c_same + c_other
-    for to, _, _, _ in peers:
+    peers = [to for to, _, _, _ in z_list + c_list] + [twin]
+    for to in peers:
         pl.semaphore_signal(barrier, inc=1, device_id=to, device_id_type=MESH)
 
     own_rows = pl.ds(me_d * i_q, i_q)
@@ -174,17 +173,32 @@
         r[me_s] = s[me_s]
         return both
 
-    def start_c(phase, s, r):
-        both = start(c_same, col_send.at[phase], col_recv.at[phase], lambda t: s.at[t], r.at[me_p], lambda t: r.at[t])
-        r[me_p] = s[me_p]
+    def start_c(phase, src_at, dst_at, own):
+        both = start(c_list, col_send.at[phase], col_recv.at[phase], src_at, dst_at(me_p), dst_at)
+        own()
         return both
 
-    def start_cc(phase, s, r):
-        sems = (col_send.at[phase], col_recv.at[phase])
-        both = start(c_same, *sems, lambda t: s.at[t], r.at[me_core, me_p], lambda t: r.at[me_core, t])
-        both += start(c_other, *sems, lambda t: s.at[t], r.at[me_core, me_p], lambda t: r.at[1 - me_core, t])
-        r[me_core, me_p] = s[me_p]
-        return both
+    def pass_on(number, k, ref_at):
+        sems = {"send_sem": twin_send.at[number, k], "recv_sem": twin_recv.at[number, k]}
+        go, come = (
+            pltpu.make_async_remote_copy(
+                src_ref=ref_at(me_core), dst_ref=ref_at(core), device_id=twin, device_id_type=MESH, **sems
+            )
+            for core in (me_core, 1 - me_core)
+        )
+        go.start()
+        started.append((go, come))
+        return (go, come)
+
+    def arrive_and_pass_on(number, both, ref):
+        passed = [pass_on(number, n_c - 1, lambda core: ref.at[core, me_p])]
+        come_from = [slot_from for _, _, slot_from, _ in c_list]
+        for at in reversed(range(len(both))):
+            both[at][1].wait_recv()
+            to, slot_from = c_list[at][0], come_from[at]
+            passed.append(pass_on(number, at, lambda core: ref.at[core, slot_from]))
+        for _, come in passed:
+            come.wait_recv()
 
     def start_d(phase, s, r):
         both = start(d_list, depth_send.at[phase], depth_recv.at[phase], lambda t: s, r.at[me_d], lambda t: r.at[t])
@@ -249,13 +263,24 @@
                 for dd in range(2) for block in range(2)
             )
             at = slice(v * LANE, (v + 1) * LANE)
-            s2[2 * h, :, at] = jnp.concatenate([a0, a1, b0, b1], axis=0).astype(BF16)
-            s2[2 * h + 1, :, at] = jnp.concatenate([a1, a0, b0, b1], axis=0).astype(BF16)
-    move = start_cc(0, s2, r2)
-    arrive(move)
+            s2b[h, :, at] = jnp.concatenate([b0, b1], axis=0).astype(BF16)
+            s2a[2 * h, :, at] = jnp.concatenate([a0, a1], axis=0).astype(BF16)
+            s2a[2 * h + 1, :, at] = jnp.concatenate([a1, a0], axis=0).astype(BF16)
+
+    def own_b():
+        r2b[me_core, me_p] = s2b[me_p // 2]
+
+    def own_a():
+        r2a[me_core, me_p] = s2a[me_p]
+
+    move = start_c(0, lambda t: s2b.at[t // 2], lambda t: r2b.at[me_core, t], own_b)
+    move_a = start_c(1, lambda t: s2a.at[t], lambda t: r2a.at[me_core, t], own_a)
+    arrive_and_pass_on(0, move, r2b)
+    arrive(move_a)
+    pass_a = pass_on(2, 0, lambda core: r2a.at[core])
 
     for core in range(2):
-        x = r2[core, :, 2 * half :, :].astype(F32)
+        x = r2b[core].astype(F32)
         for i, m in enumerate(to_matrix([lanes(x, v) for v in range(vl)], slot)):
             for dd in range(n_dd):
                 at = ((core * n_dd + dd) * i_q + i) * half
@@ -269,7 +294,7 @@
             ))
             rows.append(jnp.zeros((SLOT - k_block, full), F32))
     b_mat = jnp.concatenate(rows, axis=0).astype(BF16)
-    x = r2[me_core, :, :half, :].astype(F32)
+    x = r2a[me_core].astype(F32)[:, :half]
     a_own = jnp.concatenate(to_matrix([lanes(x, v) for v in range(vl)], slot), axis=0).astype(BF16)
     tri = lax.dot_general(a_own, b_mat, (((1,), (1,)), ((), ())), preferred_element_type=F32)
     for c, x in enumerate(from_matrix(tri.reshape(i_q, half, full), slot)):
@@ -279,14 +304,15 @@
     def rows3(t):
         return pl.ds(pl.multiple_of(t * size3, size3), size3)
 
-    move = start(
-        c_same, col_send.at[1], col_recv.at[1], lambda t: s3.at[t], r3.at[rows3(me_p)], lambda t: r3.at[rows3(t)]
-    )
-    r3[rows3(me_p), :] = s3[me_p]
-
+    def own_3():
+        r3[rows3(me_p), :] = s3[me_p]
+
+    move = start_c(2, lambda t: s3.at[t], lambda t: r3.at[rows3(t)], own_3)
+
+    arrive([pass_a])
     rows = []
     for core in range(2):
-        x = r2[core, :, : 2 * half, :].astype(F32)
+        x = r2a[core].astype(F32)
         rows += to_matrix([lanes(x, v) for v in range(vl)], slot)
     a_mat = jnp.concatenate(rows, axis=0).astype(BF16)
     arrive(move)
@@ -314,10 +340,10 @@
         return x.T.reshape(i_q, SLOT, ch)[:, :k_block, :].reshape(i_q * k_block, ch).astype(BF16)
 
     su[...] = natural(gate_val * out_proj)
-    update_move = start_d(0, su, ru)
     d_gate_pre = (cot_t * out_proj * gate_val * (1.0 - gate_val)).astype(BF16)
     d_gate = dot(w_gate[...], d_gate_pre)
     arrive(move)
+    update_move = start_d(0, su, ru)
 
     pitch = s5.shape[1]
     f5[...] = r5[...].astype(F32).reshape(n_z * pitch, LANE)
@@ -327,8 +353,12 @@
             at = slice(v * LANE, (v + 1) * LANE)
             s6[2 * h, :, at] = jnp.concatenate([t0, t1], axis=0).astype(BF16)
             s6[2 * h + 1, :, at] = jnp.concatenate([t1, t0], axis=0).astype(BF16)
-    move = start_cc(2, s6, r6)
-    arrive(move)
+
+    def own_6():
+        r6[me_core, me_p] = s6[me_p]
+
+    move = start_c(3, lambda t: s6.at[t], lambda t: r6.at[me_core, t], own_6)
+    arrive_and_pass_on(1, move, r6)
     for core in range(2):
         x = r6[core].astype(F32)
         for i, m in enumerate(to_matrix([lanes(x, v) for v in range(vl)], slot)):
@@ -350,7 +380,11 @@
     for c, x in enumerate(from_matrix(both, slot)):
         for v in range(vl):
             s8[c, :, v * LANE : (v + 1) * LANE] = x[v].astype(BF16)
-    move = start_c(3, s8, r8)
+
+    def own_8():
+        r8[me_p] = s8[me_p]
+
+    move = start_c(4, lambda t: s8.at[t], lambda t: r8.at[t], own_8)
     arrive(move)
     x = r8[...].astype(F32)
     for v in range(vl):
@@ -417,8 +451,10 @@
         vm((n_z, 2 * hz, width), BF16),
         vm((n_z, 2 * hz, width), BF16),
         vm((vl, n_z * 2 * hz, LANE), F32),
-        vm((n_c, 4 * half, width), BF16),
-        vm((2, n_c, 4 * half, width), BF16),
+        vm((n_c, 2 * half, width), BF16),
+        vm((n_c // 2, 2 * half, width), BF16),
+        vm((2, n_c, 2 * half, width), BF16),
+        vm((2, n_c, 2 * half, width), BF16),
         vm((groups, 2 * k_block * half, LANE), F32),
         vm((n_c, vl * half, LANE), F32),
         vm((n_c * vl * half, LANE), F32),
@@ -441,7 +477,7 @@
         vm((i_q * k_block, ch), BF16),
         vm((n_d, i_q * k_block, ch), BF16),
     ]
-    for phases, size in ((4, n_z), (4, 2 * n_c), (2, n_d)):
+    for phases, size in ((4, n_z), (5, n_c), (2, n_d), (3, n_c)):
         scratch += [pltpu.SemaphoreType.DMA((phases, size))] * 2
     whole = pl.BlockSpec(memory_space=pltpu.VMEM)
     return pl.pallas_call(

time: 101 us -> 96.9 us (0.959)
  Pallas kernels: 97.5 us -> 93.1 us
    pallas_call x1, Pallas kernels: 97.5 us -> 93.1 us  [shards(): pl.pallas_call(functools.partial(kernel, (n_d, n_r, n_c, n_x, i_block, k_...]
where the time goes in v3:
time: 96.9 us; the launch traced here: 96.2 us
  Pallas kernels  93.1 us (96%)
  local copies, waits for them, and re-layouts  2.47 us (3%)
    pallas_call x1, Pallas kernels, shards(): pl.pallas_call(functools.partial(kernel, (n_d, n_r, n_c, n_x, i_block, k_...  93.1 us
    unnamed x4, local copies, waits for them, and re-layouts  2.47 us

profile of v3, /device:TPU:24, one launch (start us, length us, event | category | flops | bytes accessed | tf_op | source)
XLA Modules:
  0.0 96.2 jit_solution(2032947255167372187)
XLA Ops:
  0.6 93.1 %shard_map.77 = (bf16[48,24,128]{2,1,0:T(8,128)(2,1)}, bf16[48,24,128]{2,1,0:T(8,128)(2,1)}) custom-call(s32[384]{0:T(512)} %mask_hbm.1, bf16[48,24,128]{2,1,0:T(8,128)(2,1)} %pair_hbm.1, bf16[48,24,128]{2,1,0:T(8,128)(2,1)} %cot_hbm.1, bf16[128,512]{1,0:T(8,128)(2,1)} %w_in_hbm.1, bf16[128,128]{1,0:T(8,128)(2,1)} %w_gate_hbm.1, bf16[128,128]{1,0:T(8,128)(2,1)} %w_out_hbm.1), custom_call_target="tpu_custom_call" | custom-call | tf_op jit(solution)/shard_map/pallas_call | solution.py:483
  93.7 0.0 copy-start
  93.8 1.7 %copy.10 = bf16[48,24,128]{2,1,0:T(8,128)(2,1)} copy(bf16[48,24,128]{2,1,0:T(8,128)(2,1)} %get-tuple-element.4) | data formatting | bytes 589824
  95.5 0.0 copy-done
  95.5 0.7 copy.11
Async XLA Ops:
  93.7 1.8 %copy-start = (bf16[48,24,128]{2,1,0:T(8,128)(2,1)S(1)}, bf16[48,24,128]{2,1,0:T(8,128)(2,1)}, u32[]{:S(2)}) copy-start(bf16[48,24,128]{2,1,0:T(8,128)(2,1)} %get-tuple-element.5) | copy-start | bytes 884740

commit v4 on v3

--- a/solution.py
+++ b/solution.py
@@ -75,7 +75,7 @@
     mask_hbm, pair_hbm, cot_hbm, w_in_hbm, w_gate_hbm, w_out_hbm,
     update_out, grad_out,
     mask, pair, cot, w_in, w_gate, w_out, in_sem,
-    pad, proj, s1, r1, f1, s2a, s2b, r2a, r2b, bn, s3, r3, s4, r4, s5, r5, f5, s6, r6, tgf,
+    pad, proj, s1, r1, f1, s2, r2, t2, bn, all_a, s3, r3, s4, r4, s5, r5, f5, s6, r6, t6, tgf,
     gf, s8, r8, f8, s9, r9, su, ru, sg, rg,
     z_send, z_recv, col_send, col_recv, depth_send, depth_recv, twin_send, twin_recv,
 ):
@@ -169,7 +169,12 @@
             come.wait_recv()
 
     def start_z(phase, s, r):
-        both = start(z_list, z_send.at[phase], z_recv.at[phase], lambda t: s.at[t], r.at[me_s], lambda t: r.at[t])
+        sems = (z_send.at[phase], z_recv.at[phase])
+        both = start(z_list[:9], *sems, lambda t: s.at[t], r.at[me_s], lambda t: r.at[t])
+        for pair_ in both:
+            pair_[0].wait_send()
+        del started[-9:]
+        both = both + start(z_list[9:], *sems, lambda t: s.at[t], r.at[me_s], lambda t: r.at[t])
         r[me_s] = s[me_s]
         return both
 
@@ -178,27 +183,14 @@
         own()
         return both
 
-    def pass_on(number, k, ref_at):
-        sems = {"send_sem": twin_send.at[number, k], "recv_sem": twin_recv.at[number, k]}
-        go, come = (
-            pltpu.make_async_remote_copy(
-                src_ref=ref_at(me_core), dst_ref=ref_at(core), device_id=twin, device_id_type=MESH, **sems
-            )
-            for core in (me_core, 1 - me_core)
+    def pass_on(k, src, dst):
+        go = pltpu.make_async_remote_copy(
+            src_ref=src, dst_ref=dst, send_sem=twin_send.at[k], recv_sem=twin_recv.at[k],
+            device_id=twin, device_id_type=MESH,
         )
         go.start()
-        started.append((go, come))
-        return (go, come)
-
-    def arrive_and_pass_on(number, both, ref):
-        passed = [pass_on(number, n_c - 1, lambda core: ref.at[core, me_p])]
-        come_from = [slot_from for _, _, slot_from, _ in c_list]
-        for at in reversed(range(len(both))):
-            both[at][1].wait_recv()
-            to, slot_from = c_list[at][0], come_from[at]
-            passed.append(pass_on(number, at, lambda core: ref.at[core, slot_from]))
-        for _, come in passed:
-            come.wait_recv()
+        started.append((go, go))
+        return started[-1:]
 
     def start_d(phase, s, r):
         both = start(d_list, depth_send.at[phase], depth_recv.at[phase], lambda t: s, r.at[me_d], lambda t: r.at[t])
@@ -213,11 +205,7 @@
         return pad[...].reshape(width, ch).T
 
     def pack(x):
-        parts = [lanes(x, v).reshape(n_z, hz, LANE) for v in range(vl)]
-        short = s5.shape[1] - vl * hz
-        if short:
-            parts.append(jnp.zeros((n_z, short, LANE), F32))
-        return jnp.concatenate(parts, axis=1).astype(BF16)
+        return jnp.stack([lanes(x, v).reshape(n_z, hz, LANE) for v in range(vl)], axis=1).astype(BF16)
 
     fetch[0].wait()
     x_hat, inv_std = norm_rows(padded_t(pair))
@@ -263,39 +251,40 @@
                 for dd in range(2) for block in range(2)
             )
             at = slice(v * LANE, (v + 1) * LANE)
-            s2b[h, :, at] = jnp.concatenate([b0, b1], axis=0).astype(BF16)
-            s2a[2 * h, :, at] = jnp.concatenate([a0, a1], axis=0).astype(BF16)
-            s2a[2 * h + 1, :, at] = jnp.concatenate([a1, a0], axis=0).astype(BF16)
-
-    def own_b():
-        r2b[me_core, me_p] = s2b[me_p // 2]
-
-    def own_a():
-        r2a[me_core, me_p] = s2a[me_p]
-
-    move = start_c(0, lambda t: s2b.at[t // 2], lambda t: r2b.at[me_core, t], own_b)
-    move_a = start_c(1, lambda t: s2a.at[t], lambda t: r2a.at[me_core, t], own_a)
-    arrive_and_pass_on(0, move, r2b)
-    arrive(move_a)
-    pass_a = pass_on(2, 0, lambda core: r2a.at[core])
-
-    for core in range(2):
-        x = r2b[core].astype(F32)
+            s2[2 * h, :, at] = jnp.concatenate([b0, b1, a0, a1], axis=0).astype(BF16)
+            s2[2 * h + 1, :, at] = jnp.concatenate([b0, b1, a1, a0], axis=0).astype(BF16)
+
+    def own_2():
+        r2[me_p] = s2[me_p]
+
+    b_part, a_part = slice(0, 2 * half), slice(2 * half, 4 * half)
+    move = start_c(0, lambda t: s2.at[t], lambda t: r2.at[t], own_2)
+    arrive(move)
+    pass_b = pass_on(0, r2.at[:, b_part], t2.at[:, b_part])
+    pass_a = pass_on(1, r2.at[:, a_part], t2.at[:, a_part])
+    x = r2[:, a_part, :].astype(F32)
+    a_rows = to_matrix([lanes(x, v) for v in range(vl)], slot)
+    a_own = jnp.concatenate([m[:half] for m in a_rows], axis=0).astype(BF16)
+
+    def place_b(core, ref):
+        x = ref[:, b_part, :].astype(F32)
         for i, m in enumerate(to_matrix([lanes(x, v) for v in range(vl)], slot)):
             for dd in range(n_dd):
-                at = ((core * n_dd + dd) * i_q + i) * half
+                at = (dd * i_q + i) * half
                 for g in range(groups):
-                    bn[g, at : at + half, :] = lanes(m[dd * half : (dd + 1) * half], g)
+                    bn[g, core, at : at + half, :] = lanes(m[dd * half : (dd + 1) * half], g)
+
+    place_b(me_core, r2)
+    arrive(pass_b)
+    place_b(1 - me_core, t2)
     rows = []
     for core in range(2):
         for q in range(half):
             rows.append(jnp.concatenate(
-                [bn[g, pl.ds(core * k_block * half + q, k_block, stride=half), :] for g in range(groups)], axis=-1
+                [bn[g, core, pl.ds(q, k_block, stride=half), :] for g in range(groups)], axis=-1
             ))
             rows.append(jnp.zeros((SLOT - k_block, full), F32))
     b_mat = jnp.concatenate(rows, axis=0).astype(BF16)
-    x = r2a[me_core].astype(F32)[:, :half]
-    a_own = jnp.concatenate(to_matrix([lanes(x, v) for v in range(vl)], slot), axis=0).astype(BF16)
     tri = lax.dot_general(a_own, b_mat, (((1,), (1,)), ((), ())), preferred_element_type=F32)
     for c, x in enumerate(from_matrix(tri.reshape(i_q, half, full), slot)):
         s3[c] = x.reshape(vl * half, LANE)
@@ -309,26 +298,21 @@
 
     move = start_c(2, lambda t: s3.at[t], lambda t: r3.at[rows3(t)], own_3)
 
-    arrive([pass_a])
-    rows = []
-    for core in range(2):
-        x = r2a[core].astype(F32)
-        rows += to_matrix([lanes(x, v) for v in range(vl)], slot)
-    a_mat = jnp.concatenate(rows, axis=0).astype(BF16)
+    all_a[me_core] = jnp.concatenate(a_rows, axis=0).astype(BF16)
+    arrive(pass_a)
+    x = t2[:, a_part, :].astype(F32)
+    all_a[1 - me_core] = jnp.concatenate(to_matrix([lanes(x, v) for v in range(vl)], slot), axis=0).astype(BF16)
     arrive(move)
 
     for dd in range(n_dd):
         for q in range(half):
             parts = [r3[pl.ds(dd * size3 + v * half + q, hz, stride=2 * size3), :] for v in range(vl)]
-            short = s4.shape[1] - vl * hz
-            if short:
-                parts.append(jnp.zeros((short, LANE), F32))
-            s4[dd * half + q] = jnp.concatenate(parts, axis=0).astype(BF16)
+            s4[dd * half + q] = jnp.stack(parts, axis=0).astype(BF16)
     move = start_z(1, s4, r4)
     arrive(move)
 
     x = r4[...].astype(F32)
-    tri_t = jnp.concatenate([x[:, v * hz : (v + 1) * hz, :].reshape(hid, LANE) for v in range(vl)], axis=-1)
+    tri_t = jnp.concatenate([x[:, v].reshape(hid, LANE) for v in range(vl)], axis=-1)
     y_hat, tri_std = norm_rows(tri_t)
     out_proj = dot(w_out_t, y_hat.astype(BF16))
     d_o = (cot_t * gate_val).astype(BF16)
@@ -345,7 +329,7 @@
     arrive(move)
     update_move = start_d(0, su, ru)
 
-    pitch = s5.shape[1]
+    pitch = vl * hz
     f5[...] = r5[...].astype(F32).reshape(n_z * pitch, LANE)
     for h in range(hz):
         for v in range(vl):
@@ -355,21 +339,26 @@
             s6[2 * h + 1, :, at] = jnp.concatenate([t1, t0], axis=0).astype(BF16)
 
     def own_6():
-        r6[me_core, me_p] = s6[me_p]
-
-    move = start_c(3, lambda t: s6.at[t], lambda t: r6.at[me_core, t], own_6)
-    arrive_and_pass_on(1, move, r6)
-    for core in range(2):
-        x = r6[core].astype(F32)
-        for i, m in enumerate(to_matrix([lanes(x, v) for v in range(vl)], slot)):
-            tgf[core, i] = m
-    tg_own = tgf[me_core, :, :half, :].reshape(i_q * half, full).astype(BF16)
+        r6[me_p] = s6[me_p]
+
+    move = start_c(3, lambda t: s6.at[t], lambda t: r6.at[t], own_6)
+    arrive(move)
+    pass_t = pass_on(2, r6, t6)
+    x = r6[...].astype(F32)
+    rows = to_matrix([lanes(x, v) for v in range(vl)], slot)
+    for i, m in enumerate(rows):
+        tgf[me_core, i] = m
+    tg_own = jnp.concatenate([m[:half] for m in rows], axis=0).astype(BF16)
+    grad_a = dot(tg_own, b_mat).reshape(i_q, half, full)
+    arrive(pass_t)
+    x = t6[...].astype(F32)
+    for i, m in enumerate(to_matrix([lanes(x, v) for v in range(vl)], slot)):
+        tgf[1 - me_core, i] = m
     mine = pl.ds(pl.multiple_of(me_core * (full // 2), full // 2), full // 2)
     tg_t = tgf[:, :, :, mine].reshape(2 * i_q * 2 * half, full // 2).T.astype(BF16)
-    part_b = dot(tg_t, a_mat)
+    part_b = dot(tg_t, all_a[...].reshape(2 * i_q * 2 * half, full))
     for g in range(groups):
         gf[g] = lanes(part_b, g)
-    grad_a = dot(tg_own, b_mat).reshape(i_q, half, full)
     rows = []
     for i in range(i_q):
         rows.append(grad_a[i])
@@ -436,7 +425,7 @@
     hz = hid // n_z
     full = n_c * SLOT
     groups = max(full // LANE, 1)
-    pitch = -(-vl * hz // 16) * 16
+    pitch = vl * hz
     vm = pltpu.VMEM
     scratch = [
         pltpu.SMEM(residue_mask.shape, jnp.int32),
@@ -451,20 +440,21 @@
         vm((n_z, 2 * hz, width), BF16),
         vm((n_z, 2 * hz, width), BF16),
         vm((vl, n_z * 2 * hz, LANE), F32),
-        vm((n_c, 2 * half, width), BF16),
-        vm((n_c // 2, 2 * half, width), BF16),
-        vm((2, n_c, 2 * half, width), BF16),
-        vm((2, n_c, 2 * half, width), BF16),
-        vm((groups, 2 * k_block * half, LANE), F32),
+        vm((n_c, 4 * half, width), BF16),
+        vm((n_c, 4 * half, width), BF16),
+        vm((n_c, 4 * half, width), BF16),
+        vm((groups, 2, k_block * half, LANE), F32),
+        vm((2, i_q * 2 * half, full), BF16),
         vm((n_c, vl * half, LANE), F32),
         vm((n_c * vl * half, LANE), F32),
-        vm((n_z, pitch, LANE), BF16),
-        vm((n_z, pitch, LANE), BF16),
-        vm((n_z, pitch, LANE), BF16),
-        vm((n_z, pitch, LANE), BF16),
+        vm((n_z, vl, hz, LANE), BF16),
+        vm((n_z, vl, hz, LANE), BF16),
+        vm((n_z, vl, hz, LANE), BF16),
+        vm((n_z, vl, hz, LANE), BF16),
         vm((n_z * pitch, LANE), F32),
         vm((n_c, 2 * half, width), BF16),
-        vm((2, n_c, 2 * half, width), BF16),
+        vm((n_c, 2 * half, width), BF16),
+        vm((n_c, 2 * half, width), BF16),
         vm((2, i_q, 2 * half, full), F32),
         vm((groups, full // 2, LANE), F32),
         vm((n_c, 2 * half, width), BF16),
@@ -477,8 +467,9 @@
         vm((i_q * k_block, ch), BF16),
         vm((n_d, i_q * k_block, ch), BF16),
     ]
-    for phases, size in ((4, n_z), (5, n_c), (2, n_d), (3, n_c)):
+    for phases, size in ((4, n_z), (5, n_c), (2, n_d)):
         scratch += [pltpu.SemaphoreType.DMA((phases, size))] * 2
+    scratch += [pltpu.SemaphoreType.DMA((3,))] * 2
     whole = pl.BlockSpec(memory_space=pltpu.VMEM)
     return pl.pallas_call(
         functools.partial(kernel, (n_d, n_r, n_c, n_x, i_block, k_block, ch, hid)),

time: 96.9 us -> 94 us (0.970)
  Pallas kernels: 93.1 us -> 90.3 us
    pallas_call x1, Pallas kernels: 93.1 us -> 90.3 us  [shards(): pl.pallas_call(functools.partial(kernel, (n_d, n_r, n_c, n_x, i_block, k_...]
where the time goes in v4:
time: 94 us; the launch traced here: 93.4 us
  Pallas kernels  90.3 us (96%)
  local copies, waits for them, and re-layouts  2.47 us (3%)
    pallas_call x1, Pallas kernels, shards(): pl.pallas_call(functools.partial(kernel, (n_d, n_r, n_c, n_x, i_block, k_...  90.3 us
    unnamed x4, local copies, waits for them, and re-layouts  2.47 us

profile of v4, /device:TPU:24, one launch (start us, length us, event | category | flops | bytes accessed | tf_op | source)
XLA Modules:
  0.0 93.4 jit_solution(2182137249752726322)
XLA Ops:
  0.6 90.3 %shard_map.77 = (bf16[48,24,128]{2,1,0:T(8,128)(2,1)}, bf16[48,24,128]{2,1,0:T(8,128)(2,1)}) custom-call(s32[384]{0:T(512)} %mask_hbm.1, bf16[48,24,128]{2,1,0:T(8,128)(2,1)} %pair_hbm.1, bf16[48,24,128]{2,1,0:T(8,128)(2,1)} %cot_hbm.1, bf16[128,512]{1,0:T(8,128)(2,1)} %w_in_hbm.1, bf16[128,128]{1,0:T(8,128)(2,1)} %w_gate_hbm.1, bf16[128,128]{1,0:T(8,128)(2,1)} %w_out_hbm.1), custom_call_target="tpu_custom_call" | custom-call | tf_op jit(solution)/shard_map/pallas_call | solution.py:474
  90.9 0.0 copy-start
  90.9 1.7 %copy.10 = bf16[48,24,128]{2,1,0:T(8,128)(2,1)} copy(bf16[48,24,128]{2,1,0:T(8,128)(2,1)} %get-tuple-element.4) | data formatting | bytes 589824
  92.7 0.0 copy-done
  92.7 0.7 copy.11
Async XLA Ops:
  90.9 1.8 %copy-start = (bf16[48,24,128]{2,1,0:T(8,128)(2,1)S(1)}, bf16[48,24,128]{2,1,0:T(8,128)(2,1)}, u32[]{:S(2)}) copy-start(bf16[48,24,128]{2,1,0:T(8,128)(2,1)} %get-tuple-element.5) | copy-start | bytes 884740

commit v5 on v4

--- a/solution.py
+++ b/solution.py
@@ -13,6 +13,7 @@
 SLOT = 32
 LANE = 128
 PER = LANE // SLOT
+PAD_LANES = 8
 
 
 def dot(left, right):
@@ -51,6 +52,26 @@
                 acc = y if acc is None else jnp.where(slot == c, y, acc)
             out.append(jnp.concatenate([acc[g] for g in range(groups)], axis=-1))
     return out
+
+
+def fold(a, b, chunk):
+    last, per_slot = b[-1], SLOT // PAD_LANES
+    out = []
+    for j, tile in enumerate(a):
+        moved = pltpu.roll(last, PAD_LANES * (per_slot - 1 - j), last.ndim - 1)
+        out.append(jnp.where(chunk == per_slot - 1, moved, tile))
+    return out + b[:-1]
+
+
+def unfold(tiles, chunk):
+    per_slot = SLOT // PAD_LANES
+    last = jnp.zeros_like(tiles[0])
+    a = []
+    for j, tile in enumerate(tiles[: per_slot - 1]):
+        moved = pltpu.roll(tile, LANE - PAD_LANES * (per_slot - 1 - j), tile.ndim - 1)
+        last = jnp.where(chunk == j, moved, last)
+        a.append(jnp.where(chunk == per_slot - 1, 0.0, tile))
+    return a, tiles[per_slot - 1 :] + [last]
 
 
 def from_matrix(matrix, slot):
@@ -198,6 +219,8 @@
         return both
 
     slot = lax.broadcasted_iota(jnp.int32, (1, 1, LANE), 2) // SLOT
+    chunk = lax.broadcasted_iota(jnp.int32, (1, 1, LANE), 2) % SLOT // PAD_LANES
+    chunk2 = lax.broadcasted_iota(jnp.int32, (1, LANE), 1) % SLOT // PAD_LANES
 
     def padded_t(ref):
         pad[:, :k_block, :] = ref[...].astype(F32)
@@ -229,8 +252,9 @@
         sig, val = jax.nn.sigmoid(both[:hid]), both[hid:]
         proj[2 * block] = sig
         proj[2 * block + 1] = val
-        parts.append((pair_mask * sig * val).reshape(n_z, hz, width))
-    s1[...] = jnp.concatenate(parts, axis=1).astype(BF16)
+        out = pair_mask * sig * val
+        parts.append([lanes(out, v).reshape(n_z, hz, LANE) for v in range(vl)])
+    s1[...] = jnp.stack(fold(*parts, chunk), axis=1).astype(BF16)
 
     pl.semaphore_wait(barrier, len(peers))
     move = start_z(0, s1, r1)
@@ -242,8 +266,9 @@
     arrive(move)
 
     x = r1[...].astype(F32)
+    a_tiles, b_tiles = unfold([x[:, j] for j in range(2 * vl - 1)], chunk)
     for v in range(vl):
-        f1[v] = lanes(x, v).reshape(n_z * 2 * hz, LANE)
+        f1[v] = jnp.concatenate([a_tiles[v], b_tiles[v]], axis=1).reshape(n_z * 2 * hz, LANE)
     for h in range(hz):
         for v in range(vl):
             a0, b0, a1, b1 = (
@@ -380,21 +405,19 @@
         f8[v] = lanes(x, v).reshape(n_c * 2 * half, LANE)
     for dd in range(n_dd):
         for q in range(half):
-            for v in range(vl):
-                s9[dd * half + q, :, v * LANE : (v + 1) * LANE] = jnp.concatenate(
-                    [
-                        f8[v, pl.ds((dd * 2 + block) * half + q, hz, stride=4 * half), :]
-                        for block in range(2)
-                    ],
-                    axis=0,
-                ).astype(BF16)
+            a_tiles, b_tiles = (
+                [f8[v, pl.ds((dd * 2 + block) * half + q, hz, stride=4 * half), :] for v in range(vl)]
+                for block in range(2)
+            )
+            s9[dd * half + q] = jnp.stack(fold(a_tiles, b_tiles, chunk2), axis=0).astype(BF16)
     move = start_z(3, s9, r9)
     arrive(move)
 
     d_normed = d_gate
     x = r9[...].astype(F32)
+    grads = unfold([x[:, j] for j in range(2 * vl - 1)], chunk)
     for block in range(2):
-        grad = x[:, block * hz : (block + 1) * hz, :].reshape(hid, width) * pair_mask
+        grad = jnp.concatenate([g.reshape(hid, LANE) for g in grads[block]], axis=-1) * pair_mask
         sig, val = proj[2 * block], proj[2 * block + 1]
         d_pre = (grad * val * sig * (1.0 - sig)).astype(BF16)
         d_val = (grad * sig).astype(BF16)
@@ -437,8 +460,8 @@
         pltpu.SemaphoreType.DMA((6,)),
         vm((i_q, SLOT, ch), F32),
         vm((4, hid, width), F32),
-        vm((n_z, 2 * hz, width), BF16),
-        vm((n_z, 2 * hz, width), BF16),
+        vm((n_z, 2 * vl - 1, hz, LANE), BF16),
+        vm((n_z, 2 * vl - 1, hz, LANE), BF16),
         vm((vl, n_z * 2 * hz, LANE), F32),
         vm((n_c, 4 * half, width), BF16),
         vm((n_c, 4 * half, width), BF16),
@@ -460,8 +483,8 @@
         vm((n_c, 2 * half, width), BF16),
         vm((n_c, 2 * half, width), BF16),
         vm((vl, n_c * 2 * half, LANE), F32),
-        vm((n_z, 2 * hz, width), BF16),
-        vm((n_z, 2 * hz, width), BF16),
+        vm((n_z, 2 * vl - 1, hz, LANE), BF16),
+        vm((n_z, 2 * vl - 1, hz, LANE), BF16),
         vm((i_q * k_block, ch), BF16),
         vm((n_d, i_q * k_block, ch), BF16),
         vm((i_q * k_block, ch), BF16),

time: 94 us -> 91.2 us (0.970)
  Pallas kernels: 90.3 us -> 87.8 us
    pallas_call x1, Pallas kernels: 90.3 us -> 87.8 us  [shards(): pl.pallas_call(functools.partial(kernel, (n_d, n_r, n_c, n_x, i_block, k_...]
where the time goes in v5:
time: 91.2 us; the launch traced here: 90.9 us
  Pallas kernels  87.8 us (96%)
  local copies, waits for them, and re-layouts  2.47 us (3%)
    pallas_call x1, Pallas kernels, shards(): pl.pallas_call(functools.partial(kernel, (n_d, n_r, n_c, n_x, i_block, k_...  87.8 us
    unnamed x4, local copies, waits for them, and re-layouts  2.47 us

profile of v5, /device:TPU:24, one launch (start us, length us, event | category | flops | bytes accessed | tf_op | source)
XLA Modules:
  0.0 90.9 jit_solution(2276954159436644922)
XLA Ops:
  0.6 87.8 %shard_map.77 = (bf16[48,24,128]{2,1,0:T(8,128)(2,1)}, bf16[48,24,128]{2,1,0:T(8,128)(2,1)}) custom-call(s32[384]{0:T(512)} %mask_hbm.1, bf16[48,24,128]{2,1,0:T(8,128)(2,1)} %pair_hbm.1, bf16[48,24,128]{2,1,0:T(8,128)(2,1)} %cot_hbm.1, bf16[128,512]{1,0:T(8,128)(2,1)} %w_in_hbm.1, bf16[128,128]{1,0:T(8,128)(2,1)} %w_gate_hbm.1, bf16[128,128]{1,0:T(8,128)(2,1)} %w_out_hbm.1), custom_call_target="tpu_custom_call" | custom-call | tf_op jit(solution)/shard_map/pallas_call | solution.py:497
  88.4 0.0 copy-start
  88.4 1.7 %copy.10 = bf16[48,24,128]{2,1,0:T(8,128)(2,1)} copy(bf16[48,24,128]{2,1,0:T(8,128)(2,1)} %get-tuple-element.4) | data formatting | bytes 589824
  90.2 0.0 copy-done
  90.2 0.7 copy.11
Async XLA Ops:
  88.4 1.8 %copy-start = (bf16[48,24,128]{2,1,0:T(8,128)(2,1)S(1)}, bf16[48,24,128]{2,1,0:T(8,128)(2,1)}, u32[]{:S(2)}) copy-start(bf16[48,24,128]{2,1,0:T(8,128)(2,1)} %get-tuple-element.5) | copy-start | bytes 884740

commit v6 on v5

--- a/solution.py
+++ b/solution.py
@@ -98,7 +98,7 @@
     mask, pair, cot, w_in, w_gate, w_out, in_sem,
     pad, proj, s1, r1, f1, s2, r2, t2, bn, all_a, s3, r3, s4, r4, s5, r5, f5, s6, r6, t6, tgf,
     gf, s8, r8, f8, s9, r9, su, ru, sg, rg,
-    z_send, z_recv, col_send, col_recv, depth_send, depth_recv, twin_send, twin_recv,
+    z_send, z_recv, col_send, col_recv, depth_send, depth_recv, over_send, over_recv, twin_send, twin_recv,
 ):
     n_d, n_r, n_c, n_x, i_block, k_block, ch, hid = dims
     n_zh, n_dd, n_y = n_r // 2, n_d // 2, n_c // n_x
@@ -149,10 +149,14 @@
     c_list = [
         c_peer(ox, oy) + (c_peer(-ox, -oy)[1], k) for k, (ox, oy) in enumerate(c_offsets) if (ox, oy) != (0, 0)
     ]
+    x_list = []
+    for k, (ox, oy) in enumerate(c_offsets):
+        to, slot_to = c_peer(ox, oy)
+        x_list.append(({**to, "row": me_zh * 2 + 1 - me_core}, slot_to, c_peer(-ox, -oy)[1], k))
     twin = {"row": me_zh * 2 + 1 - me_core}
 
     barrier = pltpu.get_barrier_semaphore()
-    peers = [to for to, _, _, _ in z_list + c_list] + [twin]
+    peers = [to for to, _, _, _ in z_list + c_list + x_list]
     for to in peers:
         pl.semaphore_signal(barrier, inc=1, device_id=to, device_id_type=MESH)
 
@@ -283,9 +287,12 @@
         r2[me_p] = s2[me_p]
 
     b_part, a_part = slice(0, 2 * half), slice(2 * half, 4 * half)
+    pass_b = start(
+        x_list, over_send.at[0], over_recv.at[0],
+        lambda t: s2.at[t, b_part], t2.at[me_p, b_part], lambda t: t2.at[t, b_part],
+    )
     move = start_c(0, lambda t: s2.at[t], lambda t: r2.at[t], own_2)
     arrive(move)
-    pass_b = pass_on(0, r2.at[:, b_part], t2.at[:, b_part])
     pass_a = pass_on(1, r2.at[:, a_part], t2.at[:, a_part])
     x = r2[:, a_part, :].astype(F32)
     a_rows = to_matrix([lanes(x, v) for v in range(vl)], slot)
@@ -366,9 +373,9 @@
     def own_6():
         r6[me_p] = s6[me_p]
 
+    pass_t = start(x_list, over_send.at[1], over_recv.at[1], lambda t: s6.at[t], t6.at[me_p], lambda t: t6.at[t])
     move = start_c(3, lambda t: s6.at[t], lambda t: r6.at[t], own_6)
     arrive(move)
-    pass_t = pass_on(2, r6, t6)
     x = r6[...].astype(F32)
     rows = to_matrix([lanes(x, v) for v in range(vl)], slot)
     for i, m in enumerate(rows):
@@ -450,6 +457,10 @@
     groups = max(full // LANE, 1)
     pitch = vl * hz
     vm = pltpu.VMEM
+    operands = [
+        pltpu.with_memory_space_constraint(v, pltpu.HBM)
+        for v in (residue_mask, pair, cotangent, w_in, w_gate, w_out)
+    ]
     scratch = [
         pltpu.SMEM(residue_mask.shape, jnp.int32),
         vm((i_q, k_block, ch), BF16),
@@ -492,6 +503,7 @@
     ]
     for phases, size in ((4, n_z), (5, n_c), (2, n_d)):
         scratch += [pltpu.SemaphoreType.DMA((phases, size))] * 2
+    scratch += [pltpu.SemaphoreType.DMA((2, n_c))] * 2
     scratch += [pltpu.SemaphoreType.DMA((3,))] * 2
     whole = pl.BlockSpec(memory_space=pltpu.VMEM)
     return pl.pallas_call(
@@ -501,9 +513,9 @@
         out_specs=(whole, whole),
         scratch_shapes=scratch,
         compiler_params=pltpu.CompilerParams(
-            collective_id=0, has_side_effects=True, vmem_limit_bytes=60 * 1024 * 1024
+            collective_id=0, has_side_effects=True, vmem_limit_bytes=40 * 1024 * 1024
         ),
-    )(residue_mask, pair, cotangent, w_in, w_gate, w_out)
+    )(*operands)
 
 
 def solution(mesh):

time: 91.2 us -> 88 us (0.965)
  Pallas kernels: 87.8 us -> 85.7 us
  local copies, waits for them, and re-layouts: 2.47 us -> 1.43 us
    pallas_call x1, Pallas kernels: 87.8 us -> 85.7 us  [shards(): pl.pallas_call(functools.partial(kernel, (n_d, n_r, n_c, n_x, i_block, k_...]
    unnamed x4 -> x2, local copies, waits for them, and re-layouts: 2.47 us -> 1.43 us
where the time goes in v6:
time: 88 us; the launch traced here: 87.8 us
  Pallas kernels  85.7 us (97%)
  local copies, waits for them, and re-layouts  1.43 us (2%)
    pallas_call x1, Pallas kernels, shards(): pl.pallas_call(functools.partial(kernel, (n_d, n_r, n_c, n_x, i_block, k_...  85.7 us

profile of v6, /device:TPU:24, one launch (start us, length us, event | category | flops | bytes accessed | tf_op | source)
XLA Modules:
  0.0 87.8 jit_solution(18402824389883419212)
XLA Ops:
  0.6 85.7 %shard_map.77 = (bf16[48,24,128]{2,1,0:T(8,128)(2,1)S(1)}, bf16[48,24,128]{2,1,0:T(8,128)(2,1)S(1)}) custom-call(s32[384]{0:T(512)} %mask_hbm.1, bf16[48,24,128]{2,1,0:T(8,128)(2,1)} %pair_hbm.1, bf16[48,24,128]{2,1,0:T(8,128)(2,1)} %cot_hbm.1, bf16[128,512]{1,0:T(8,128)(2,1)} %w_in_hbm.1, bf16[128,128]{1,0:T(8,128)(2,1)} %w_gate_hbm.1, ...), custom_call_target="tpu_custom_call" | custom-call | tf_op jit(solution)/shard_map/pallas_call | solution.py:509
  86.4 0.7 copy.10
  87.1 0.7 copy.11

commit v7 on v6

--- a/solution.py
+++ b/solution.py
@@ -96,7 +96,7 @@
     mask_hbm, pair_hbm, cot_hbm, w_in_hbm, w_gate_hbm, w_out_hbm,
     update_out, grad_out,
     mask, pair, cot, w_in, w_gate, w_out, in_sem,
-    pad, proj, s1, r1, f1, s2, r2, t2, bn, all_a, s3, r3, s4, r4, s5, r5, f5, s6, r6, t6, tgf,
+    pad, proj, s1, r1, f1, s2, r2, t2, bn, all_a, s3, r3, f3, s4, r4, s5, r5, f5, s6, r6, t6, tgf,
     gf, s8, r8, f8, s9, r9, su, ru, sg, rg,
     z_send, z_recv, col_send, col_recv, depth_send, depth_recv, over_send, over_recv, twin_send, twin_recv,
 ):
@@ -319,16 +319,13 @@
     b_mat = jnp.concatenate(rows, axis=0).astype(BF16)
     tri = lax.dot_general(a_own, b_mat, (((1,), (1,)), ((), ())), preferred_element_type=F32)
     for c, x in enumerate(from_matrix(tri.reshape(i_q, half, full), slot)):
-        s3[c] = x.reshape(vl * half, LANE)
+        s3[c] = x.astype(BF16)
     size3 = vl * half
 
-    def rows3(t):
-        return pl.ds(pl.multiple_of(t * size3, size3), size3)
-
     def own_3():
-        r3[rows3(me_p), :] = s3[me_p]
-
-    move = start_c(2, lambda t: s3.at[t], lambda t: r3.at[rows3(t)], own_3)
+        r3[me_p] = s3[me_p]
+
+    move = start_c(2, lambda t: s3.at[t], lambda t: r3.at[t], own_3)
 
     all_a[me_core] = jnp.concatenate(a_rows, axis=0).astype(BF16)
     arrive(pass_a)
@@ -336,9 +333,10 @@
     all_a[1 - me_core] = jnp.concatenate(to_matrix([lanes(x, v) for v in range(vl)], slot), axis=0).astype(BF16)
     arrive(move)
 
+    f3[...] = r3[...].astype(F32).reshape(n_c * size3, LANE)
     for dd in range(n_dd):
         for q in range(half):
-            parts = [r3[pl.ds(dd * size3 + v * half + q, hz, stride=2 * size3), :] for v in range(vl)]
+            parts = [f3[pl.ds(dd * size3 + v * half + q, hz, stride=2 * size3), :] for v in range(vl)]
             s4[dd * half + q] = jnp.stack(parts, axis=0).astype(BF16)
     move = start_z(1, s4, r4)
     arrive(move)
@@ -359,7 +357,6 @@
     d_gate_pre = (cot_t * out_proj * gate_val * (1.0 - gate_val)).astype(BF16)
     d_gate = dot(w_gate[...], d_gate_pre)
     arrive(move)
-    update_move = start_d(0, su, ru)
 
     pitch = vl * hz
     f5[...] = r5[...].astype(F32).reshape(n_z * pitch, LANE)
@@ -376,6 +373,7 @@
     pass_t = start(x_list, over_send.at[1], over_recv.at[1], lambda t: s6.at[t], t6.at[me_p], lambda t: t6.at[t])
     move = start_c(3, lambda t: s6.at[t], lambda t: r6.at[t], own_6)
     arrive(move)
+    update_move = start_d(0, su, ru)
     x = r6[...].astype(F32)
     rows = to_matrix([lanes(x, v) for v in range(vl)], slot)
     for i, m in enumerate(rows):
@@ -479,7 +477,8 @@
         vm((n_c, 4 * half, width), BF16),
         vm((groups, 2, k_block * half, LANE), F32),
         vm((2, i_q * 2 * half, full), BF16),
-        vm((n_c, vl * half, LANE), F32),
+        vm((n_c, vl, half, LANE), BF16),
+        vm((n_c, vl, half, LANE), BF16),
         vm((n_c * vl * half, LANE), F32),
         vm((n_z, vl, hz, LANE), BF16),
         vm((n_z, vl, hz, LANE), BF16),

time: 88 us -> 86.5 us (0.983)
  Pallas kernels: 85.7 us -> 84.2 us
    pallas_call x1, Pallas kernels: 85.7 us -> 84.2 us  [shards(): pl.pallas_call(functools.partial(kernel, (n_d, n_r, n_c, n_x, i_block, k_...]
where the time goes in v7:
time: 86.5 us; the launch traced here: 86.3 us
  Pallas kernels  84.2 us (97%)
  local copies, waits for them, and re-layouts  1.43 us (2%)
    pallas_call x1, Pallas kernels, shards(): pl.pallas_call(functools.partial(kernel, (n_d, n_r, n_c, n_x, i_block, k_...  84.2 us

profile of v7, /device:TPU:24, one launch (start us, length us, event | category | flops | bytes accessed | tf_op | source)
XLA Modules:
  0.0 86.3 jit_solution(2358233648503250174)
XLA Ops:
  0.6 84.2 %shard_map.77 = (bf16[48,24,128]{2,1,0:T(8,128)(2,1)S(1)}, bf16[48,24,128]{2,1,0:T(8,128)(2,1)S(1)}) custom-call(s32[384]{0:T(512)} %mask_hbm.1, bf16[48,24,128]{2,1,0:T(8,128)(2,1)} %pair_hbm.1, bf16[48,24,128]{2,1,0:T(8,128)(2,1)} %cot_hbm.1, bf16[128,512]{1,0:T(8,128)(2,1)} %w_in_hbm.1, bf16[128,128]{1,0:T(8,128)(2,1)} %w_gate_hbm.1, ...), custom_call_target="tpu_custom_call" | custom-call | tf_op jit(solution)/shard_map/pallas_call | solution.py:508
  84.9 0.7 copy.10
  85.6 0.7 copy.11

commit v8 on v7

--- a/solution.py
+++ b/solution.py
@@ -388,7 +388,7 @@
     tg_t = tgf[:, :, :, mine].reshape(2 * i_q * 2 * half, full // 2).T.astype(BF16)
     part_b = dot(tg_t, all_a[...].reshape(2 * i_q * 2 * half, full))
     for g in range(groups):
-        gf[g] = lanes(part_b, g)
+        gf[g, : full // 2] = lanes(part_b, g)
     rows = []
     for i in range(i_q):
         rows.append(grad_a[i])
@@ -489,7 +489,7 @@
         vm((n_c, 2 * half, width), BF16),
         vm((n_c, 2 * half, width), BF16),
         vm((2, i_q, 2 * half, full), F32),
-        vm((groups, full // 2, LANE), F32),
+        vm((groups, full // 2 + SLOT, LANE), F32),
         vm((n_c, 2 * half, width), BF16),
         vm((n_c, 2 * half, width), BF16),
         vm((vl, n_c * 2 * half, LANE), F32),

time: 86.5 us -> 86.6 us (level)
  no operation moved by 1% of the time
where the time goes in v8:
time: 86.6 us; the launch traced here: 86.3 us
  Pallas kernels  84.2 us (97%)
  local copies, waits for them, and re-layouts  1.43 us (2%)
    pallas_call x1, Pallas kernels, shards(): pl.pallas_call(functools.partial(kernel, (n_d, n_r, n_c, n_x, i_block, k_...  84.2 us

profile of v8, /device:TPU:24, one launch (start us, length us, event | category | flops | bytes accessed | tf_op | source)
XLA Modules:
  0.0 86.3 jit_solution(3020074770087490419)
XLA Ops:
  0.6 84.2 %shard_map.77 = (bf16[48,24,128]{2,1,0:T(8,128)(2,1)S(1)}, bf16[48,24,128]{2,1,0:T(8,128)(2,1)S(1)}) custom-call(s32[384]{0:T(512)} %mask_hbm.1, bf16[48,24,128]{2,1,0:T(8,128)(2,1)} %pair_hbm.1, bf16[48,24,128]{2,1,0:T(8,128)(2,1)} %cot_hbm.1, bf16[128,512]{1,0:T(8,128)(2,1)} %w_in_hbm.1, bf16[128,128]{1,0:T(8,128)(2,1)} %w_gate_hbm.1, ...), custom_call_target="tpu_custom_call" | custom-call | tf_op jit(solution)/shard_map/pallas_call | solution.py:508
  84.8 0.7 copy.10
  85.6 0.7 copy.11
